TPU v7x, 128 devices: a whole 4x4x4 slice. The times are simulated.
128 devices in a mesh: dp: 2 (over core), context: 8 (over y, z_lo), tensor: 8 (over x, z_hi).
Axes of the slice: x: 4, y: 4, z: 4 (z_hi: 2, z_lo: 2; z = z_hi * 2 + z_lo), core: 2. Of those that a mesh axis runs over, the one named last changes fastest.
Arguments:
- queries: bfloat16 [32768, 8192], P(('dp', 'context', 'tensor')), parts along dimension 0, may hold values from -5 to 5
- rotated_key_rows: bfloat16 [32768, 1024], P(('dp', 'context', 'tensor')), parts along dimension 0, may hold values from -5 to 5
- stored_value_rows: bfloat16 [32768, 1024], P(('dp', 'context', 'tensor')), parts along dimension 0, may hold values from -5 to 5
- doc_lengths: int32 [32], P('dp'), parts along dimension 0, may hold values from 1 to 2048, 16384 in all
- block_order: int32 [128], P('dp'), parts along dimension 0, may hold values from 0 to 63, each once
Outputs:
- attended: bfloat16 [32768, 8192], P(('dp', 'context', 'tensor')), parts along dimension 0
There are 2 independent parts, one for each index of `dp`. A program takes and returns all parts, laid end to end along the dimension named above; each array names one. Nothing has to cross between parts.
Inputs may be any that keep to these rules, and one draw needn't show every extreme that they name: `doc_lengths`: the 16 lengths sum to 16384; the longest is exactly 2048. `block_order`: A permutation of the 64 sequence blocks of 256 tokens.
All inputs are finite; a program needn't handle non-finite values.
Results may differ from a plain program's by a relative error of at most 0.0045.
Values may be sent and summed in bfloat16 or wider, within the bound.
No kernel may reach another device: no remote copies, remote signals or barrier semaphores. Data moves between devices by JAX's collectives and lax.ppermute only.
A program may use at most 128 MiB of HBM per device.

v0:
```python
import math

import jax
import jax.numpy as jnp
from jax import lax
from jax.sharding import PartitionSpec as P

QUERY_HEADS = 64
KEY_VALUE_HEADS = 8
HEAD_SIZE = 128


NEG_BIG = -1e30


def doc_index(doc_lengths, sequence_length):
    doc_ends = jnp.cumsum(doc_lengths)
    places = jnp.arange(sequence_length, dtype=jnp.int32)
    return jnp.sum((places[:, None] >= doc_ends[None, :]).astype(jnp.int32), axis=1)


def inverse_order(block_order):
    count_of_blocks = block_order.shape[0]
    places = jnp.arange(count_of_blocks, dtype=jnp.int32)
    matches = (block_order[None, :] == places[:, None]).astype(jnp.int32)
    return jnp.sum(matches * places[None, :], axis=1)


def attend(q_tiles, q_starts, key_seq, value_seq, doc_ids, key_tile):
    tile_count, tile_rows, q_heads, head_width = q_tiles.shape
    sequence_length, k_heads, _ = key_seq.shape
    query_group_width = q_heads // k_heads
    score_scale = 1.0 / math.sqrt(head_width)
    key_count = sequence_length // key_tile
    longest = sequence_length // 8

    def one_tile(tile_input):
        q_tile, start = tile_input
        q_grouped = q_tile.reshape(tile_rows, k_heads, query_group_width, head_width)
        q_pos = start + jnp.arange(tile_rows, dtype=jnp.int32)
        q_doc = lax.dynamic_slice_in_dim(doc_ids, start, tile_rows)
        last_pos = start + tile_rows - 1
        first_tile = jnp.maximum(start - longest + 1, 0) // key_tile
        end_tile = jnp.minimum(last_pos // key_tile + 1, key_count)

        def key_step(tile_index, state):
            row_peak, row_total, accum_out = state
            k_start = tile_index * key_tile
            k_block = lax.dynamic_slice_in_dim(key_seq, k_start, key_tile)
            v_block = lax.dynamic_slice_in_dim(value_seq, k_start, key_tile)
            k_pos = k_start + jnp.arange(key_tile, dtype=jnp.int32)
            k_doc = lax.dynamic_slice_in_dim(doc_ids, k_start, key_tile)
            visible = (k_pos[None, :] <= q_pos[:, None]) & (k_doc[None, :] == q_doc[:, None])
            scores = (
                jnp.einsum("rkgd,skd->rkgs", q_grouped, k_block, preferred_element_type=jnp.float32)
                * score_scale
            )
            scores = jnp.where(visible[:, None, None, :], scores, -jnp.inf)
            new_peak = jnp.maximum(row_peak, jnp.max(scores, axis=-1))
            weights = jnp.exp(scores - new_peak[..., None])
            factor = jnp.exp(row_peak - new_peak)
            row_total = factor * row_total + jnp.sum(weights, axis=-1)
            mixed = jnp.einsum(
                "rkgs,skd->rkgd",
                weights.astype(jnp.bfloat16),
                v_block,
                preferred_element_type=jnp.float32,
            )
            accum_out = factor[..., None] * accum_out + mixed
            return (new_peak, row_total, accum_out)

        initial = (
            jnp.full((tile_rows, k_heads, query_group_width), NEG_BIG, jnp.float32),
            jnp.zeros((tile_rows, k_heads, query_group_width), jnp.float32),
            jnp.zeros((tile_rows, k_heads, query_group_width, head_width), jnp.float32),
        )
        row_peak, row_total, accum_out = lax.fori_loop(first_tile, end_tile, key_step, initial)
        attention_output = (accum_out / row_total[..., None]).astype(jnp.bfloat16)
        return attention_output.reshape(tile_rows, q_heads * head_width)

    return lax.map(one_tile, (q_tiles, q_starts))


def body(queries, rotated_key_rows, stored_value_rows, doc_lengths, block_order):
    tok_rows = queries.shape[0]
    context_count = lax.axis_size("context")
    ten_count = lax.axis_size("tensor")
    devices = context_count * ten_count
    sequence_length = tok_rows * devices
    doc_ids = doc_index(doc_lengths, sequence_length)
    inverse_permutation = inverse_order(block_order)
    key_tile = max(min(1024, sequence_length), sequence_length // 16)
    per_device = QUERY_HEADS // devices
    key_value_share = KEY_VALUE_HEADS // context_count
    q_mine = lax.all_to_all(queries, ("context", "tensor"), split_axis=1, concat_axis=0, tiled=True)
    k_group, v_group = (
        lax.all_to_all(rotated_key_rows, "context", split_axis=1, concat_axis=0, tiled=True),
        lax.all_to_all(stored_value_rows, "context", split_axis=1, concat_axis=0, tiled=True),
    )
    k_every, v_every = (
        lax.all_gather(k_group, "tensor", axis=0, tiled=True),
        lax.all_gather(v_group, "tensor", axis=0, tiled=True),
    )
    row_block = inverse_permutation % ten_count * context_count + inverse_permutation // ten_count

    def order_heads(gathered):
        blocks = gathered.reshape(devices, tok_rows, key_value_share, HEAD_SIZE)
        return jnp.take(blocks, row_block, axis=0).reshape(sequence_length, 1, HEAD_SIZE)

    key_seq = order_heads(k_every)
    value_seq = order_heads(v_every)
    query_sequence = jnp.take(
        q_mine.reshape(devices, tok_rows, per_device * HEAD_SIZE), inverse_permutation, axis=0
    )
    tile_rows = key_tile // per_device
    q_tiles = query_sequence.reshape(sequence_length // tile_rows, tile_rows, per_device, HEAD_SIZE)
    starts = jnp.arange(sequence_length // tile_rows, dtype=jnp.int32) * tile_rows
    out_seq = attend(q_tiles, starts, key_seq, value_seq, doc_ids, key_tile)
    out_seq = out_seq.reshape(devices, tok_rows, per_device * HEAD_SIZE)
    out_stored = jnp.take(out_seq, block_order, axis=0).reshape(
        sequence_length, per_device * HEAD_SIZE
    )
    return lax.all_to_all(
        out_stored, ("context", "tensor"), split_axis=0, concat_axis=1, tiled=True
    )


def solution(mesh):
    in_specs = (
        P(("dp", "context", "tensor"), None),
        P(("dp", "context", "tensor"), None),
        P(("dp", "context", "tensor"), None),
        P("dp"),
        P("dp"),
    )
    out_specs = P(("dp", "context", "tensor"), None)
    return jax.shard_map(body, mesh=mesh, in_specs=in_specs, out_specs=out_specs, check_vma=False)
```

profile of v0, /device:TPU:0, one launch (start us, length us, event | category | flops | bytes accessed | tf_op | source)
XLA Modules:
  0.0 640.0 jit_solution(13462602750728954406)
XLA Ops:
  7.8 15.4 %all_to_all.70 = bf16[256,8,128]{0,2,1:T(8,128)(2,1)S(1)} all-to-all(bf16[256,8,128]{0,2,1:T(8,128)(2,1)S(1)} %bitcast.112), channel_id=1, replica_groups=mesh['dp'=2,'context'=8,'tensor'=8] {'context'}, dimensions={1} | all-to-all | bytes 1048576 | tf_op jit(solution)/shard_map/all_to_all | solution.py:97
  25.6 11.6 %all_to_all.71 = bf16[256,8,128]{0,2,1:T(8,128)(2,1)S(1)} all-to-all(bf16[256,8,128]{0,2,1:T(8,128)(2,1)S(1)} %bitcast.113), channel_id=1, replica_groups=mesh['dp'=2,'context'=8,'tensor'=8] {'context'}, dimensions={1} | all-to-all | bytes 1048576 | tf_op jit(solution)/shard_map/all_to_all | solution.py:98
  44.5 6.4 copy.23
  50.9 9.5 %all-to-all-start = ((bf16[256,64,128]{2,0,1:T(8,128)(2,1)}), bf16[256,64,128]{2,0,1:T(8,128)(2,1)}, u32[]{:S(2)}, u32[]{:S(2)}) async-start(bf16[256,64,128]{2,0,1:T(8,128)(2,1)} %copy.23), calls=%async_computation | async-start | bytes 8388608 | tf_op jit(solution)/shard_map/all_to_all | solution.py:95
  61.2 55.4 %all-to-all-done = bf16[256,64,128]{2,0,1:T(8,128)(2,1)} async-done(((bf16[256,64,128]{2,0,1:T(8,128)(2,1)}), bf16[256,64,128]{2,0,1:T(8,128)(2,1)}, u32[]{:S(2)}, u32[]{:S(2)}) %all-to-all-start) | async-done | bytes 4194336 | tf_op jit(solution)/shard_map/all_to_all | solution.py:95
  126.5 15.7 %all-gather.3.cloned.1.call-done = bf16[16384,128]{1,0:T(8,128)(2,1)} async-done(((bf16[2048,128]{1,0:T(8,128)(2,1)}), bf16[16384,128]{1,0:T(8,128)(2,1)}) %all-gather.3.cloned.1.call-update) | async-done | bytes 4194320 | tf_op jit(solution)/shard_map/all_gather | solution.py:101
  147.5 66.4 %all-gather.5.cloned.1.call-done = bf16[16384,128]{1,0:T(8,128)(2,1)} async-done(((bf16[2048,128]{1,0:T(8,128)(2,1)}), bf16[16384,128]{1,0:T(8,128)(2,1)}) %all-gather.5.cloned.1.call-update) | async-done | bytes 4194320 | tf_op jit(solution)/shard_map/all_gather | solution.py:102
  225.1 329.0 %while.59 = (s32[]{:T(128)}, bf16[16,1024,128]{2,1,0:T(8,128)(2,1)}, s32[16]{0:T(128)S(1)}, s32[16384]{0:T(1024)S(1)}, bf16[16,1024,1,128]{3,1,2,0:T(8,128)(2,1)...) while((s32[]{:T(128)}, ...), condition=%wide.region_8.11_spmd, body=%wide.region_3.0_spmd.sunk | while | flops 547885056 | bytes 17421668 | solution.py:81
  240.5 10.7 %while.60 = (s32[]{:T(128)}, f32[1024,1,1]{0,2,1:T(1,128)S(1)}, f32[1024,1,1]{0,2,1:T(1,128)S(1)}, f32[1024,1,1,128]{0,3,2,1:T(8,128)S(1)}, s32[]{:T(128)}, /*in...) while((s32[]{:T(128)}, f32[1024,1,1]{0,2,1:T(1,128)S(1)}, ...), condition=%wide.region_7.9_spmd.clone, body=%wide.region_4.8_spmd.clone.sunk | while | flops 547622912 | bytes 14516431 | solution.py:77
  256.7 16.1 %while.60 = (s32[]{:T(128)}, f32[1024,1,1]{0,2,1:T(1,128)S(1)}, f32[1024,1,1]{0,2,1:T(1,128)S(1)}, f32[1024,1,1,128]{0,3,2,1:T(8,128)S(1)}, s32[]{:T(128)}, /*in...) while((s32[]{:T(128)}, f32[1024,1,1]{0,2,1:T(1,128)S(1)}, ...), condition=%wide.region_7.9_spmd.clone, body=%wide.region_4.8_spmd.clone.sunk | while | flops 547622912 | bytes 14516431 | solution.py:77
  278.3 16.1 %while.60 = (s32[]{:T(128)}, f32[1024,1,1]{0,2,1:T(1,128)S(1)}, f32[1024,1,1]{0,2,1:T(1,128)S(1)}, f32[1024,1,1,128]{0,3,2,1:T(8,128)S(1)}, s32[]{:T(128)}, /*in...) while((s32[]{:T(128)}, f32[1024,1,1]{0,2,1:T(1,128)S(1)}, ...), condition=%wide.region_7.9_spmd.clone, body=%wide.region_4.8_spmd.clone.sunk | while | flops 547622912 | bytes 14516431 | solution.py:77
  299.8 16.1 %while.60 = (s32[]{:T(128)}, f32[1024,1,1]{0,2,1:T(1,128)S(1)}, f32[1024,1,1]{0,2,1:T(1,128)S(1)}, f32[1024,1,1,128]{0,3,2,1:T(8,128)S(1)}, s32[]{:T(128)}, /*in...) while((s32[]{:T(128)}, f32[1024,1,1]{0,2,1:T(1,128)S(1)}, ...), condition=%wide.region_7.9_spmd.clone, body=%wide.region_4.8_spmd.clone.sunk | while | flops 547622912 | bytes 14516431 | solution.py:77
  321.4 16.1 %while.60 = (s32[]{:T(128)}, f32[1024,1,1]{0,2,1:T(1,128)S(1)}, f32[1024,1,1]{0,2,1:T(1,128)S(1)}, f32[1024,1,1,128]{0,3,2,1:T(8,128)S(1)}, s32[]{:T(128)}, /*in...) while((s32[]{:T(128)}, f32[1024,1,1]{0,2,1:T(1,128)S(1)}, ...), condition=%wide.region_7.9_spmd.clone, body=%wide.region_4.8_spmd.clone.sunk | while | flops 547622912 | bytes 14516431 | solution.py:77
  343.0 16.1 %while.60 = (s32[]{:T(128)}, f32[1024,1,1]{0,2,1:T(1,128)S(1)}, f32[1024,1,1]{0,2,1:T(1,128)S(1)}, f32[1024,1,1,128]{0,3,2,1:T(8,128)S(1)}, s32[]{:T(128)}, /*in...) while((s32[]{:T(128)}, f32[1024,1,1]{0,2,1:T(1,128)S(1)}, ...), condition=%wide.region_7.9_spmd.clone, body=%wide.region_4.8_spmd.clone.sunk | while | flops 547622912 | bytes 14516431 | solution.py:77
  364.5 16.1 %while.60 = (s32[]{:T(128)}, f32[1024,1,1]{0,2,1:T(1,128)S(1)}, f32[1024,1,1]{0,2,1:T(1,128)S(1)}, f32[1024,1,1,128]{0,3,2,1:T(8,128)S(1)}, s32[]{:T(128)}, /*in...) while((s32[]{:T(128)}, f32[1024,1,1]{0,2,1:T(1,128)S(1)}, ...), condition=%wide.region_7.9_spmd.clone, body=%wide.region_4.8_spmd.clone.sunk | while | flops 547622912 | bytes 14516431 | solution.py:77
  386.1 16.1 %while.60 = (s32[]{:T(128)}, f32[1024,1,1]{0,2,1:T(1,128)S(1)}, f32[1024,1,1]{0,2,1:T(1,128)S(1)}, f32[1024,1,1,128]{0,3,2,1:T(8,128)S(1)}, s32[]{:T(128)}, /*in...) while((s32[]{:T(128)}, f32[1024,1,1]{0,2,1:T(1,128)S(1)}, ...), condition=%wide.region_7.9_spmd.clone, body=%wide.region_4.8_spmd.clone.sunk | while | flops 547622912 | bytes 14516431 | solution.py:77
  407.7 16.1 %while.60 = (s32[]{:T(128)}, f32[1024,1,1]{0,2,1:T(1,128)S(1)}, f32[1024,1,1]{0,2,1:T(1,128)S(1)}, f32[1024,1,1,128]{0,3,2,1:T(8,128)S(1)}, s32[]{:T(128)}, /*in...) while((s32[]{:T(128)}, f32[1024,1,1]{0,2,1:T(1,128)S(1)}, ...), condition=%wide.region_7.9_spmd.clone, body=%wide.region_4.8_spmd.clone.sunk | while | flops 547622912 | bytes 14516431 | solution.py:77
  429.2 16.1 %while.60 = (s32[]{:T(128)}, f32[1024,1,1]{0,2,1:T(1,128)S(1)}, f32[1024,1,1]{0,2,1:T(1,128)S(1)}, f32[1024,1,1,128]{0,3,2,1:T(8,128)S(1)}, s32[]{:T(128)}, /*in...) while((s32[]{:T(128)}, f32[1024,1,1]{0,2,1:T(1,128)S(1)}, ...), condition=%wide.region_7.9_spmd.clone, body=%wide.region_4.8_spmd.clone.sunk | while | flops 547622912 | bytes 14516431 | solution.py:77
  450.8 16.1 %while.60 = (s32[]{:T(128)}, f32[1024,1,1]{0,2,1:T(1,128)S(1)}, f32[1024,1,1]{0,2,1:T(1,128)S(1)}, f32[1024,1,1,128]{0,3,2,1:T(8,128)S(1)}, s32[]{:T(128)}, /*in...) while((s32[]{:T(128)}, f32[1024,1,1]{0,2,1:T(1,128)S(1)}, ...), condition=%wide.region_7.9_spmd.clone, body=%wide.region_4.8_spmd.clone.sunk | while | flops 547622912 | bytes 14516431 | solution.py:77
  472.4 16.1 %while.60 = (s32[]{:T(128)}, f32[1024,1,1]{0,2,1:T(1,128)S(1)}, f32[1024,1,1]{0,2,1:T(1,128)S(1)}, f32[1024,1,1,128]{0,3,2,1:T(8,128)S(1)}, s32[]{:T(128)}, /*in...) while((s32[]{:T(128)}, f32[1024,1,1]{0,2,1:T(1,128)S(1)}, ...), condition=%wide.region_7.9_spmd.clone, body=%wide.region_4.8_spmd.clone.sunk | while | flops 547622912 | bytes 14516431 | solution.py:77
  493.9 16.1 %while.60 = (s32[]{:T(128)}, f32[1024,1,1]{0,2,1:T(1,128)S(1)}, f32[1024,1,1]{0,2,1:T(1,128)S(1)}, f32[1024,1,1,128]{0,3,2,1:T(8,128)S(1)}, s32[]{:T(128)}, /*in...) while((s32[]{:T(128)}, f32[1024,1,1]{0,2,1:T(1,128)S(1)}, ...), condition=%wide.region_7.9_spmd.clone, body=%wide.region_4.8_spmd.clone.sunk | while | flops 547622912 | bytes 14516431 | solution.py:77
  515.5 16.1 %while.60 = (s32[]{:T(128)}, f32[1024,1,1]{0,2,1:T(1,128)S(1)}, f32[1024,1,1]{0,2,1:T(1,128)S(1)}, f32[1024,1,1,128]{0,3,2,1:T(8,128)S(1)}, s32[]{:T(128)}, /*in...) while((s32[]{:T(128)}, f32[1024,1,1]{0,2,1:T(1,128)S(1)}, ...), condition=%wide.region_7.9_spmd.clone, body=%wide.region_4.8_spmd.clone.sunk | while | flops 547622912 | bytes 14516431 | solution.py:77
  537.1 16.1 %while.60 = (s32[]{:T(128)}, f32[1024,1,1]{0,2,1:T(1,128)S(1)}, f32[1024,1,1]{0,2,1:T(1,128)S(1)}, f32[1024,1,1,128]{0,3,2,1:T(8,128)S(1)}, s32[]{:T(128)}, /*in...) while((s32[]{:T(128)}, f32[1024,1,1]{0,2,1:T(1,128)S(1)}, ...), condition=%wide.region_7.9_spmd.clone, body=%wide.region_4.8_spmd.clone.sunk | while | flops 547622912 | bytes 14516431 | solution.py:77
  561.9 58.6 %all_to_all.72 = bf16[64,256,128]{2,1,0:T(8,128)(2,1)} all-to-all(bf16[64,256,128]{2,1,0:T(8,128)(2,1)S(1)} %broadcast_select_fusion), channel_id=1, replica_groups=mesh['dp'=2,'context'=8,'tensor'=8] {'context','tensor'}, dimensions={0} | all-to-all | bytes 8388608 | tf_op jit(solution)/shard_map/all_to_all | solution.py:123
  (541 shorter events, 343.2 us)
Async XLA Ops:
  6.5 135.7 %all-gather.3.cloned.1.call-start = ((), (), s32[]{:S(2)}) async-start(), calls=%async_computation.4 | async-start | bytes 4718592 | tf_op jit(solution)/shard_map/all_gather | solution.py:101
  24.3 189.6 %all-gather.5.cloned.1.call-start = ((), (), s32[]{:S(2)}) async-start(), calls=%async_computation.5 | async-start | bytes 4718592 | tf_op jit(solution)/shard_map/all_gather | solution.py:102
  50.9 9.5 %copy-start = (s32[16]{0:T(128)S(1)}, s32[16]{0:T(128)}, u32[]{:S(2)}) copy-start(s32[16]{0:T(128)} %param.16) | copy-start | bytes 196
  50.9 9.8 %copy-start.1 = (s32[64]{0:T(128)S(1)}, s32[64]{0:T(128)}, u32[]{:S(2)}) copy-start(s32[64]{0:T(128)} %param.17) | copy-start | bytes 772
  50.9 65.8 %all-to-all-start = ((bf16[256,64,128]{2,0,1:T(8,128)(2,1)}), bf16[256,64,128]{2,0,1:T(8,128)(2,1)}, u32[]{:S(2)}, u32[]{:S(2)}) async-start(bf16[256,64,128]{2,0,1:T(8,128)(2,1)} %copy.23), calls=%async_computation | async-start | bytes 8388608 | tf_op jit(solution)/shard_map/all_to_all | solution.py:95
Sparse Core Ops, SparseCore 0:
  24.4 117.8 all-gather.2
  144.6 69.2 all-gather.4
where the time goes:
time: 645 us; the launch traced here: 640 us
  matrix products  182 us (28%)
  waiting for transfers between devices  138 us (21%)
  local copies, waits for them, and re-layouts  92.6 us (14%)
  blocking collectives  85.6 us (13%)
  other arithmetic  69.2 us (11%)
  loops' own time  49.7 us (8%)
  between operations  13.5 us (2%)
  starting transfers between devices  9.52 us (1%)
    dot_general x45, matrix products, key_step(): jnp.einsum('rkgd,skd->rkgs', q_grouped, k_block, preferred_element_type=j...  97.4 us
    dot_general x45, matrix products, key_step(): jnp.einsum('rkgs,skd->rkgd', weights.astype(jnp.bfloat16), v_block, prefe...  85 us
    all_gather x1, waiting for transfers between devices, body(): lax.all_gather(v_group, 'tensor', axis=0, tiled=True)  66.4 us
    all_to_all x1, blocking collectives, body(): lax.all_to_all(out_stored, ('context', 'tensor'), split_axis=0, concat_ax...  58.6 us
    all_to_all x1, waiting for transfers between devices, body(): lax.all_to_all(queries, ('context', 'tensor'), split_axis=1, concat_axis=...  55.4 us
    another operation x1, loops' own time, attend(): return lax.map(one_tile, (q_tiles, q_starts))  46.3 us
    reduce_sum x45, other arithmetic, key_step(): row_total = factor * row_total + jnp.sum(weights, axis=-1)  28 us
    add x45, other arithmetic, one_tile(): q_pos = start + jnp.arange(tile_rows, dtype=jnp.int32)  25.3 us
  transfers between devices with their start and end apart: 3, of which 3 were waited for; matrix products, arithmetic and copies ran while one was open for 5% of the time, Pallas kernels for 0%

commit v1 on v0

v1 whole, which is shorter than its diff:
```python
import functools
import math

import jax
import jax.numpy as jnp
from jax import lax
from jax.experimental import pallas as pl
from jax.experimental.pallas import tpu as pltpu
from jax.sharding import PartitionSpec as P

HEAD = 128
GROUP = 8
KV_HEADS = 8
DOCS = 16
HIDDEN = -1e30
CHUNKS = 4


def gather_kernel(past, order_ref, recv_ref, out_ref, inverse):
    blocks = order_ref.shape[0]

    def note(j, carry):
        inverse[order_ref[j]] = j
        return carry

    lax.fori_loop(0, blocks, note, 0)

    def fill(d, carry):
        s = order_ref[d]
        for u in range(past // 2):
            a = recv_ref[inverse[jnp.maximum(s - 1 - 2 * u, 0)], 0].astype(jnp.float32)
            b = recv_ref[inverse[jnp.maximum(s - 2 - 2 * u, 0)], 0].astype(jnp.float32)
            out_ref[d, u, 0] = jnp.concatenate([a[:8], b[:8]], axis=0).astype(jnp.bfloat16)
            out_ref[d, u, 1] = jnp.concatenate([a[8:], b[8:]], axis=0).astype(jnp.bfloat16)
        return carry

    lax.fori_loop(0, blocks, fill, 0)


def gather_windows(chunk, past, block_order, recv):
    blocks = block_order.shape[0]
    return pl.pallas_call(
        functools.partial(gather_kernel, past),
        out_shape=jax.ShapeDtypeStruct((blocks, past // 2, 2, 16, HEAD), jnp.bfloat16),
        grid_spec=pltpu.PrefetchScalarGridSpec(
            num_scalar_prefetch=1,
            grid=(1,),
            in_specs=[pl.BlockSpec((blocks, 1, 16, HEAD), lambda i, o: (0, chunk, 0, 0))],
            out_specs=pl.BlockSpec((blocks, past // 2, 2, 16, HEAD), lambda i, o: (0, 0, 0, 0, 0)),
            scratch_shapes=[pltpu.SMEM((blocks,), jnp.int32)],
        ),
        compiler_params=pltpu.CompilerParams(vmem_limit_bytes=24 << 20),
        cost_estimate=pl.CostEstimate(flops=0, bytes_accessed=3 << 20, transcendentals=0),
        name="gather_windows",
    )(block_order, recv)


def attend_kernel(q_ref, k_own, v_own, window, q_doc, k_doc, *rest):
    out_ref, keys, values = rest[-3:]
    rows = q_ref.shape[0]
    past_keys = keys.shape[0] - rows
    keys[:past_keys, :HEAD] = window[:, :, 0].reshape(past_keys, HEAD)
    keys[past_keys:, :HEAD] = k_own[...]
    keys[:, HEAD:] = k_doc[...]
    values[:past_keys, :HEAD] = window[:, :, 1].reshape(past_keys, HEAD)
    values[past_keys:, :HEAD] = v_own[...]
    values[:, HEAD:] = jnp.ones((past_keys + rows, HEAD), jnp.bfloat16)
    scale = math.log2(math.e) / math.sqrt(HEAD)
    causal = lax.broadcasted_iota(jnp.int32, (rows, rows), 0) >= lax.broadcasted_iota(
        jnp.int32, (rows, rows), 1
    )

    def one_head(g, carry):
        columns = pl.ds(pl.multiple_of(g * HEAD, HEAD), HEAD)
        q = jnp.concatenate([q_ref[:, columns], q_doc[...]], axis=1)
        dims = (((1,), (1,)), ((), ()))
        before = lax.dot_general(
            q, keys[:past_keys, :], dims, preferred_element_type=jnp.float32
        )
        own = lax.dot_general(q, keys[past_keys:, :], dims, preferred_element_type=jnp.float32)
        own = jnp.where(causal, own, HIDDEN)
        peak = jnp.maximum(
            jnp.max(before, axis=1, keepdims=True), jnp.max(own, axis=1, keepdims=True)
        )
        w_before = jnp.exp2((before - peak) * scale).astype(jnp.bfloat16)
        w_own = jnp.exp2((own - peak) * scale).astype(jnp.bfloat16)
        total = jnp.dot(w_before, values[:past_keys, :], preferred_element_type=jnp.float32)
        total += jnp.dot(w_own, values[past_keys:, :], preferred_element_type=jnp.float32)
        out_ref[:, columns] = (total[:, :HEAD] / total[:, HEAD:]).astype(jnp.bfloat16)
        return carry

    lax.fori_loop(0, GROUP, one_head, 0)


def attend(chunk, queries, own_keys, own_values, window, q_doc, k_doc, attended):
    rows, width = queries.shape
    halves = KV_HEADS // CHUNKS
    sources, pairs = window.shape[:2]
    per_half = sources // halves
    total_keys = per_half * pairs * 16 + rows
    head = lambda i: (0, CHUNKS * i + chunk)
    whole = lambda i: (0, 0)
    in_specs = [
        pl.BlockSpec((rows, GROUP * HEAD), head),
        pl.BlockSpec((rows, HEAD), head),
        pl.BlockSpec((rows, HEAD), head),
        pl.BlockSpec((per_half, pairs, 2, 16, HEAD), lambda i: (i, 0, 0, 0, 0)),
        pl.BlockSpec((rows, HEAD), whole),
        pl.BlockSpec((total_keys, HEAD), whole),
    ]
    operands = [queries, own_keys, own_values, window, q_doc, k_doc]
    aliases = {}
    if attended is not None:
        in_specs.append(pl.BlockSpec(memory_space=pl.ANY))
        operands.append(attended)
        aliases = {6: 0}
    pairs_done = halves * GROUP * rows * total_keys
    return pl.pallas_call(
        attend_kernel,
        out_shape=jax.ShapeDtypeStruct((rows, width), jnp.bfloat16),
        grid=(halves,),
        in_specs=in_specs,
        out_specs=pl.BlockSpec((rows, GROUP * HEAD), head),
        scratch_shapes=[
            pltpu.VMEM((total_keys, 2 * HEAD), jnp.bfloat16),
            pltpu.VMEM((total_keys, 2 * HEAD), jnp.bfloat16),
        ],
        input_output_aliases=aliases,
        compiler_params=pltpu.CompilerParams(vmem_limit_bytes=40 << 20),
        cost_estimate=pl.CostEstimate(
            flops=pairs_done * 2 * 4 * HEAD, bytes_accessed=5 << 20, transcendentals=pairs_done
        ),
        name="attend",
    )(*operands)


def body(queries, rotated_key_rows, stored_value_rows, doc_lengths, block_order):
    rows = queries.shape[0]
    axes = ("context", "tensor")
    blocks = block_order.shape[0]
    halves = KV_HEADS // CHUNKS
    groups = blocks // halves
    thin = rows // groups
    past = 8

    def sliced(x):
        x = x.reshape(groups, thin, halves, CHUNKS, HEAD).transpose(2, 0, 3, 1, 4)
        return x.reshape(blocks, CHUNKS, thin, HEAD)

    pieces = jnp.concatenate([sliced(rotated_key_rows), sliced(stored_value_rows)], axis=2)
    recv = lax.all_to_all(pieces, axes, split_axis=0, concat_axis=0, tiled=True)

    me = lax.axis_index("context") * lax.axis_size("tensor") + lax.axis_index("tensor")
    place = block_order[me]
    ends = jnp.cumsum(doc_lengths)
    far = jnp.full((HEAD - DOCS,), 1 << 30, jnp.int32)
    end = jnp.concatenate([ends, far])[None, :]
    start = jnp.concatenate([ends - doc_lengths, far])[None, :]
    q_pos = (place * rows + jnp.arange(rows, dtype=jnp.int32))[:, None]
    q_doc = ((q_pos >= start) & (q_pos < end)).astype(jnp.bfloat16)
    key = jnp.arange(past * rows, dtype=jnp.int32)
    within = key % 16
    slot = 2 * (key // 16 % (past // 2)) + within // thin
    key_block = place - 1 - slot
    key_pos = key_block * rows + key // (16 * (past // 2)) * thin + within % thin
    key_pos = jnp.concatenate([jnp.where(key_block >= 0, key_pos, -1)[:, None], q_pos])
    k_doc = jnp.where((key_pos >= start) & (key_pos < end), 0.0, HIDDEN).astype(jnp.bfloat16)

    attended = None
    windows = []
    for chunk in range(CHUNKS):
        sends = gather_windows(chunk, past, block_order, recv)
        windows.append(lax.all_to_all(sends, axes, split_axis=0, concat_axis=0, tiled=True))
    for chunk in range(CHUNKS):
        attended = attend(
            chunk, queries, rotated_key_rows, stored_value_rows, windows[chunk], q_doc, k_doc, attended
        )
    return attended


def solution(mesh):
    rows = P(("dp", "context", "tensor"), None)
    return jax.shard_map(
        body,
        mesh=mesh,
        in_specs=(rows, rows, rows, P("dp"), P("dp")),
        out_specs=rows,
        check_vma=False,
    )
```

time: 645 us -> 260 us (0.40)
  matrix products: 182 us -> 0 us
  Pallas kernels: 0 us -> 126 us
  local copies, waits for them, and re-layouts: 92.6 us -> 9.29 us
  waiting for transfers between devices: 138 us -> 67.6 us
  other arithmetic: 69.2 us -> 2.39 us
  blocking collectives: 85.6 us -> 30.1 us
  loops' own time: 49.7 us -> 0 us
  starting transfers between devices: 9.52 us -> 21.9 us
  between operations: 13.5 us -> 1.28 us
    dot_general x90 -> x0, matrix products: 182 us -> none  [the longest x45 97.4 us: key_step(): jnp.einsum('rkgd,skd->rkgs', q_grouped, k_block, preferred_element_type=j...]
    pallas_call x0 -> x8, Pallas kernels: none -> 126 us  [the longest x4 110 us: attend(): pl.pallas_call(attend_kernel, out_shape=jax.ShapeDtypeStruct((rows, width...]
    all_gather x2 -> x0, waiting for transfers between devices: 82.1 us -> none  [the longest x1 66.4 us: body(): lax.all_gather(v_group, 'tensor', axis=0, tiled=True)]
    all_to_all x3 -> x1, blocking collectives: 85.6 us -> 30.1 us  [body(): recv = lax.all_to_all(pieces, axes, split_axis=0, concat_axis=0, tiled=True)]
    another operation x17 -> x0, loops' own time: 49.7 us -> none  [the longest x1 46.3 us: attend(): return lax.map(one_tile, (q_tiles, q_starts))]
    reduce_sum x47 -> x0, other arithmetic: 28.5 us -> none  [the longest x45 28 us: key_step(): row_total = factor * row_total + jnp.sum(weights, axis=-1)]
    add x90 -> x2, other arithmetic: 26.3 us -> 0.02 us  [body(): q_pos = (place * rows + jnp.arange(rows, dtype=jnp.int32))[:, None]]
    all_to_all x5 -> x0, local copies, waits for them, and re-layouts: 21.1 us -> none  [the longest x2 12.7 us: body(): lax.all_to_all(out_stored, ('context', 'tensor'), split_axis=0, concat_ax...]
  transfers between devices with their start and end apart: 3 -> 4, of which waited for: 3 -> 3; matrix products, arithmetic and copies ran while one was open for 5% -> 1% of each run, Pallas kernels for 0% -> 36%
where the time goes in v1:
time: 260 us; the launch traced here: 259 us
  Pallas kernels  126 us (48%)
  waiting for transfers between devices  67.6 us (26%)
  blocking collectives  30.1 us (12%)
  starting transfers between devices  21.9 us (8%)
  local copies, waits for them, and re-layouts  9.29 us (4%)
    pallas_call x4, Pallas kernels, attend(): pl.pallas_call(attend_kernel, out_shape=jax.ShapeDtypeStruct((rows, width...  110 us
    all_to_all x4, waiting for transfers between devices, body(): lax.all_to_all(sends, axes, split_axis=0, concat_axis=0, tiled=True)  67.6 us
    all_to_all x1, blocking collectives, body(): recv = lax.all_to_all(pieces, axes, split_axis=0, concat_axis=0, tiled=True)  30.1 us
    all_to_all x4, starting transfers between devices, body(): lax.all_to_all(sends, axes, split_axis=0, concat_axis=0, tiled=True)  21.9 us
    pallas_call x4, Pallas kernels, gather_windows(): pl.pallas_call(functools.partial(gather_kernel, past), out_shape=jax.Shap...  15.5 us
    unnamed x18, local copies, waits for them, and re-layouts  6.47 us
  transfers between devices with their start and end apart: 4, of which 3 were waited for; matrix products, arithmetic and copies ran while one was open for 1% of the time, Pallas kernels for 36%

profile of v1, /device:TPU:0, one launch (start us, length us, event | category | flops | bytes accessed | tf_op | source)
XLA Modules:
  0.0 258.6 jit_solution(2187575718090364872)
XLA Ops:
  0.0 1.1 copy.13
  1.1 1.1 copy.12
  2.4 30.1 %all_to_all.25.recv_ref = bf16[64,4,16,128]{3,2,1,0:T(8,128)(2,1)S(1)} all-to-all(bf16[64,4,16,128]{3,2,1,0:T(8,128)(2,1)S(1)} %pad_maximum_fusion), channel_id=1, replica_groups=mesh['dp'=2,'context'=8,'tensor'=8] {'context','tensor'}, dimensions={0} | all-to-all | bytes 2097152 | tf_op jit(solution)/shard_map/all_to_all | solution.py:151
  32.5 3.9 %gather_windows.7 = bf16[64,4,2,16,128]{4,3,2,1,0:T(8,128)(2,1)} custom-call(s32[64]{0:T(128)S(1)} %copy-done.5, bf16[64,4,16,128]{3,2,1,0:T(8,128)(2,1)S(1)} %all_to_all.25.recv_ref), custom_call_target="tpu_custom_call" | custom-call | bytes 3145728 | tf_op jit(solution)/shard_map/gather_windows/pallas_call | solution.py:42
  36.4 5.1 %all-to-all-start.4 = ((bf16[64,4,2,16,128]{4,3,2,1,0:T(8,128)(2,1)}), bf16[64,4,2,16,128]{4,3,2,1,0:T(8,128)(2,1)S(1)}, u32[]{:S(2)}, u32[]{:S(2)}) async-start(bf16[64,4,2,16,128]{4,3,2,1,0:T(8,128)(2,1)} %gather_windows.7), calls=%async_computation.4 | async-start | bytes 4194304 | tf_op jit(solution)/shard_map/all_to_all | solution.py:173
  41.4 3.9 %gather_windows.6 = bf16[64,4,2,16,128]{4,3,2,1,0:T(8,128)(2,1)} custom-call(s32[64]{0:T(128)S(1)} %copy-done.5, bf16[64,4,16,128]{3,2,1,0:T(8,128)(2,1)S(1)} %all_to_all.25.recv_ref), custom_call_target="tpu_custom_call" | custom-call | bytes 3145728 | tf_op jit(solution)/shard_map/gather_windows/pallas_call | solution.py:42
  45.3 24.6 %all-to-all-done.4.window = bf16[64,4,2,16,128]{4,3,2,1,0:T(8,128)(2,1)S(1)} async-done(((bf16[64,4,2,16,128]{4,3,2,1,0:T(8,128)(2,1)}), bf16[64,4,2,16,128]{4,3,2,1,0:T(8,128)(2,1)S(1)}, u32[]{:S(2)}, u32[]{:S(2)}) %all-to-all-start.4) | async-done | bytes 2097184 | tf_op jit(solution)/shard_map/all_to_all | solution.py:173
  69.9 5.6 %all-to-all-start.3 = ((bf16[64,4,2,16,128]{4,3,2,1,0:T(8,128)(2,1)}), bf16[64,4,2,16,128]{4,3,2,1,0:T(8,128)(2,1)}, u32[]{:S(2)}, u32[]{:S(2)}) async-start(bf16[64,4,2,16,128]{4,3,2,1,0:T(8,128)(2,1)} %gather_windows.6), calls=%async_computation.3 | async-start | bytes 4194304 | tf_op jit(solution)/shard_map/all_to_all | solution.py:173
  75.5 3.9 %gather_windows.5 = bf16[64,4,2,16,128]{4,3,2,1,0:T(8,128)(2,1)} custom-call(s32[64]{0:T(128)S(1)} %copy-done.5, bf16[64,4,16,128]{3,2,1,0:T(8,128)(2,1)S(1)} %all_to_all.25.recv_ref), custom_call_target="tpu_custom_call" | custom-call | bytes 3145728 | tf_op jit(solution)/shard_map/gather_windows/pallas_call | solution.py:42
  79.4 24.0 %all-to-all-done.3.window = bf16[64,4,2,16,128]{4,3,2,1,0:T(8,128)(2,1)} async-done(((bf16[64,4,2,16,128]{4,3,2,1,0:T(8,128)(2,1)}), bf16[64,4,2,16,128]{4,3,2,1,0:T(8,128)(2,1)}, u32[]{:S(2)}, u32[]{:S(2)}) %all-to-all-start.3) | async-done | bytes 2097184 | tf_op jit(solution)/shard_map/all_to_all | solution.py:173
  103.4 5.6 %all-to-all-start.2 = ((bf16[64,4,2,16,128]{4,3,2,1,0:T(8,128)(2,1)}), bf16[64,4,2,16,128]{4,3,2,1,0:T(8,128)(2,1)}, u32[]{:S(2)}, u32[]{:S(2)}) async-start(bf16[64,4,2,16,128]{4,3,2,1,0:T(8,128)(2,1)} %gather_windows.5), calls=%async_computation.2 | async-start | bytes 4194304 | tf_op jit(solution)/shard_map/all_to_all | solution.py:173
  109.0 0.6 dynamic_slice.3
  111.2 1.8 select_convert_fusion.k_doc
  113.0 3.9 %gather_windows.4 = bf16[64,4,2,16,128]{4,3,2,1,0:T(8,128)(2,1)} custom-call(s32[64]{0:T(128)S(1)} %copy-done.5, bf16[64,4,16,128]{3,2,1,0:T(8,128)(2,1)S(1)} %all_to_all.25.recv_ref), custom_call_target="tpu_custom_call" | custom-call | bytes 3145728 | tf_op jit(solution)/shard_map/gather_windows/pallas_call | solution.py:42
  116.9 19.0 %all-to-all-done.2.window = bf16[64,4,2,16,128]{4,3,2,1,0:T(8,128)(2,1)} async-done(((bf16[64,4,2,16,128]{4,3,2,1,0:T(8,128)(2,1)}), bf16[64,4,2,16,128]{4,3,2,1,0:T(8,128)(2,1)}, u32[]{:S(2)}, u32[]{:S(2)}) %all-to-all-start.2) | async-done | bytes 2097184 | tf_op jit(solution)/shard_map/all_to_all | solution.py:173
  135.9 5.7 %all-to-all-start.1 = ((bf16[64,4,2,16,128]{4,3,2,1,0:T(8,128)(2,1)}), bf16[64,4,2,16,128]{4,3,2,1,0:T(8,128)(2,1)}, u32[]{:S(2)}, u32[]{:S(2)}) async-start(bf16[64,4,2,16,128]{4,3,2,1,0:T(8,128)(2,1)} %gather_windows.4), calls=%async_computation.1 | async-start | bytes 4194304 | tf_op jit(solution)/shard_map/all_to_all | solution.py:173
  141.7 1.0 copy-done.1
  142.7 1.0 copy-done.3
  143.8 2.2 copy-done.6
  145.9 26.7 %attend.4.rest_0_ = bf16[256,8192]{1,0:T(8,128)(2,1)} custom-call(bf16[256,8192]{1,0:T(8,128)(2,1)S(1)} %copy-done.6, bf16[256,1024]{1,0:T(8,128)(2,1)S(1)} %copy-done.1, bf16[256,1024]{1,0:T(8,128)(2,1)S(1)} %copy-done.3, bf16[64,4,2,16,128]{4,3,2,1,0:T(8,128)(2,1)S(1)} %all-to-all-done.4.window, bf16[256,128]{1,0:T(8,128)(2,1)S(1)} %and_convert_fusion.q_doc, ...), custom_call_target="tpu_custom_call" | custom-call | flops 9663676416 | bytes 5242880 | tf_op jit(solution)/shard_map/attend/pallas_call | solution.py:118
  172.6 27.8 %attend.5.rest_0_ = bf16[256,8192]{1,0:T(8,128)(2,1)} custom-call(bf16[256,8192]{1,0:T(8,128)(2,1)S(1)} %copy-done.6, bf16[256,1024]{1,0:T(8,128)(2,1)S(1)} %copy-done.1, bf16[256,1024]{1,0:T(8,128)(2,1)S(1)} %copy-done.3, bf16[64,4,2,16,128]{4,3,2,1,0:T(8,128)(2,1)} %all-to-all-done.3.window, ...), custom_call_target="tpu_custom_call", output_to_operand_aliasing={{}: (6, {})} | custom-call | flops 9663676416 | bytes 5242880 | tf_op jit(solution)/shard_map/attend/pallas_call | solution.py:118
  200.5 28.1 %attend.6.rest_0_ = bf16[256,8192]{1,0:T(8,128)(2,1)} custom-call(bf16[256,8192]{1,0:T(8,128)(2,1)S(1)} %copy-done.6, bf16[256,1024]{1,0:T(8,128)(2,1)S(1)} %copy-done.1, bf16[256,1024]{1,0:T(8,128)(2,1)S(1)} %copy-done.3, bf16[64,4,2,16,128]{4,3,2,1,0:T(8,128)(2,1)} %all-to-all-done.2.window, ...), custom_call_target="tpu_custom_call", output_to_operand_aliasing={{}: (6, {})} | custom-call | flops 9663676416 | bytes 5242880 | tf_op jit(solution)/shard_map/attend/pallas_call | solution.py:118
  228.6 2.2 copy-done.7
  230.8 27.8 %attend.7 = bf16[256,8192]{1,0:T(8,128)(2,1)} custom-call(bf16[256,8192]{1,0:T(8,128)(2,1)S(1)} %copy-done.7, bf16[256,1024]{1,0:T(8,128)(2,1)S(1)} %copy-done.2, bf16[256,1024]{1,0:T(8,128)(2,1)S(1)} %copy-done.4, bf16[64,4,2,16,128]{4,3,2,1,0:T(8,128)(2,1)} %all-to-all-done.1.window, ...), custom_call_target="tpu_custom_call", output_to_operand_aliasing={{}: (6, {})} | custom-call | flops 9663676416 | bytes 5242880 | tf_op jit(solution)/shard_map/attend/pallas_call | solution.py:118
  (27 shorter events, 0.7 us)
Async XLA Ops:
  2.2 30.3 %copy-start.5 = (s32[64]{0:T(128)S(1)}, s32[64]{0:T(128)}, u32[]{:S(2)}) copy-start(s32[64]{0:T(128)} %order_ref.7) | copy-start | bytes 772
  36.4 33.6 %all-to-all-start.4 = ((bf16[64,4,2,16,128]{4,3,2,1,0:T(8,128)(2,1)}), bf16[64,4,2,16,128]{4,3,2,1,0:T(8,128)(2,1)S(1)}, u32[]{:S(2)}, u32[]{:S(2)}) async-start(bf16[64,4,2,16,128]{4,3,2,1,0:T(8,128)(2,1)} %gather_windows.7), calls=%async_computation.4 | async-start | bytes 4194304 | tf_op jit(solution)/shard_map/all_to_all | solution.py:173
  69.9 33.4 %all-to-all-start.3 = ((bf16[64,4,2,16,128]{4,3,2,1,0:T(8,128)(2,1)}), bf16[64,4,2,16,128]{4,3,2,1,0:T(8,128)(2,1)}, u32[]{:S(2)}, u32[]{:S(2)}) async-start(bf16[64,4,2,16,128]{4,3,2,1,0:T(8,128)(2,1)} %gather_windows.6), calls=%async_computation.3 | async-start | bytes 4194304 | tf_op jit(solution)/shard_map/all_to_all | solution.py:173
  79.4 31.3 %copy-start.8 = (s32[16]{0:T(128)S(1)}, s32[16]{0:T(128)}, u32[]{:S(2)}) copy-start(s32[16]{0:T(128)} %param.8) | copy-start | bytes 196
  103.4 32.5 %all-to-all-start.2 = ((bf16[64,4,2,16,128]{4,3,2,1,0:T(8,128)(2,1)}), bf16[64,4,2,16,128]{4,3,2,1,0:T(8,128)(2,1)}, u32[]{:S(2)}, u32[]{:S(2)}) async-start(bf16[64,4,2,16,128]{4,3,2,1,0:T(8,128)(2,1)} %gather_windows.5), calls=%async_computation.2 | async-start | bytes 4194304 | tf_op jit(solution)/shard_map/all_to_all | solution.py:173
  116.9 24.7 %copy-start = (bf16[2304,128]{1,0:T(8,128)(2,1)S(1)}, bf16[2304,128]{1,0:T(8,128)(2,1)}, u32[]{:S(2)}) copy-start(bf16[2304,128]{1,0:T(8,128)(2,1)} %select_convert_fusion.k_doc) | copy-start | bytes 1769476
  135.9 92.7 %all-to-all-start.1 = ((bf16[64,4,2,16,128]{4,3,2,1,0:T(8,128)(2,1)}), bf16[64,4,2,16,128]{4,3,2,1,0:T(8,128)(2,1)}, u32[]{:S(2)}, u32[]{:S(2)}) async-start(bf16[64,4,2,16,128]{4,3,2,1,0:T(8,128)(2,1)} %gather_windows.4), calls=%async_computation.1 | async-start | bytes 4194304 | tf_op jit(solution)/shard_map/all_to_all | solution.py:173
  141.7 1.0 copy-start.1
  142.7 1.0 copy-start.3
  143.8 2.2 copy-start.6
  200.5 28.1 %copy-start.2 = (bf16[256,1024]{1,0:T(8,128)(2,1)S(1)}, bf16[256,1024]{1,0:T(8,128)(2,1)}, u32[]{:S(2)}) copy-start(bf16[256,1024]{1,0:T(8,128)(2,1)} %k_own.7) | copy-start | bytes 1572868
  200.5 28.1 %copy-start.4 = (bf16[256,1024]{1,0:T(8,128)(2,1)S(1)}, bf16[256,1024]{1,0:T(8,128)(2,1)}, u32[]{:S(2)}) copy-start(bf16[256,1024]{1,0:T(8,128)(2,1)} %v_own.7) | copy-start | bytes 1572868
  228.6 2.2 copy-start.7

commit v2 on v1

v2 whole, which is shorter than its diff:
```python
import functools
import math

import jax
import jax.numpy as jnp
from jax import lax
from jax.experimental import pallas as pl
from jax.experimental.pallas import tpu as pltpu
from jax.sharding import PartitionSpec as P

HEAD = 128
GROUP = 8
KV_HEADS = 8
DOCS = 16
HIDDEN = -1e30
UNITS = 4
CHUNKS = ((0, 3), (3, 1))
STACK = 4


def pieces_kernel(k_ref, v_ref, out_ref):
    thin = out_ref.shape[2] // 2
    tall = 2 * thin
    groups = out_ref.shape[0] // 2

    def some_rows(r, carry):
        rows = pl.ds(pl.multiple_of(r * tall, tall), tall)
        for h in range(KV_HEADS):
            k = k_ref[rows, h * HEAD : (h + 1) * HEAD].astype(jnp.float32)
            v = v_ref[rows, h * HEAD : (h + 1) * HEAD].astype(jnp.float32)
            for half in range(2):
                part = slice(half * thin, (half + 1) * thin)
                both = jnp.concatenate([k[part], v[part]], axis=0).astype(jnp.bfloat16)
                out_ref[h // UNITS * groups + 2 * r + half, h % UNITS] = both
        return carry

    lax.fori_loop(0, k_ref.shape[0] // tall, some_rows, 0)


def cut_pieces(own_keys, own_values, blocks):
    rows = own_keys.shape[0]
    thin = rows * KV_HEADS // (UNITS * blocks)
    return pl.pallas_call(
        pieces_kernel,
        out_shape=jax.ShapeDtypeStruct((blocks, UNITS, 2 * thin, HEAD), jnp.bfloat16),
        compiler_params=pltpu.CompilerParams(vmem_limit_bytes=24 << 20),
        cost_estimate=pl.CostEstimate(flops=0, bytes_accessed=2 << 20, transcendentals=0),
        name="cut_pieces",
    )(own_keys, own_values)


def gather_kernel(past, order_ref, recv_ref, out_ref, inverse):
    blocks = order_ref.shape[0]
    together = 4

    @pl.when(pl.program_id(0) == 0)
    def _():
        for j in range(blocks):
            inverse[order_ref[j]] = j

    def fill(i, carry):
        for d in range(together):
            d = i * together + d
            s = order_ref[d]
            for u in range(past // 2):
                a = recv_ref[inverse[jnp.maximum(s - 1 - 2 * u, 0)], 0].astype(jnp.float32)
                b = recv_ref[inverse[jnp.maximum(s - 2 - 2 * u, 0)], 0].astype(jnp.float32)
                out_ref[d, 0, u, 0] = jnp.concatenate([a[:8], b[:8]], axis=0).astype(jnp.bfloat16)
                out_ref[d, 0, u, 1] = jnp.concatenate([a[8:], b[8:]], axis=0).astype(jnp.bfloat16)
        return carry

    lax.fori_loop(0, blocks // together, fill, 0)


def gather_windows(first, units, past, block_order, recv):
    blocks = block_order.shape[0]
    pairs = past // 2
    return pl.pallas_call(
        functools.partial(gather_kernel, past),
        out_shape=jax.ShapeDtypeStruct((blocks, units, pairs, 2, 16, HEAD), jnp.bfloat16),
        grid_spec=pltpu.PrefetchScalarGridSpec(
            num_scalar_prefetch=1,
            grid=(units,),
            in_specs=[pl.BlockSpec((blocks, 1, 16, HEAD), lambda i, o: (0, first + i, 0, 0))],
            out_specs=pl.BlockSpec(
                (blocks, 1, pairs, 2, 16, HEAD), lambda i, o: (0, i, 0, 0, 0, 0)
            ),
            scratch_shapes=[pltpu.SMEM((blocks,), jnp.int32)],
        ),
        compiler_params=pltpu.CompilerParams(vmem_limit_bytes=24 << 20),
        cost_estimate=pl.CostEstimate(flops=0, bytes_accessed=units << 21, transcendentals=0),
        name="gather_windows",
    )(block_order, recv)


def attend_kernel(q_ref, k_own, v_own, window, q_doc, k_doc, *rest):
    out_ref, keys, values, stacked, scores_a, scores_b, peak_a, peak_b = rest[-8:]
    rows = q_ref.shape[0]
    total_keys = keys.shape[0]
    past_keys = total_keys - rows
    tall = STACK * rows
    keys[:past_keys, :HEAD] = window[:, 0, :, 0].reshape(past_keys, HEAD)
    keys[past_keys:, :HEAD] = k_own[...]
    keys[:, HEAD:] = k_doc[...]
    values[:past_keys, :HEAD] = window[:, 0, :, 1].reshape(past_keys, HEAD)
    values[past_keys:, :HEAD] = v_own[...]
    values[:, HEAD:] = jnp.ones((total_keys, HEAD), jnp.bfloat16)
    for g in range(GROUP):
        stacked[g * rows : (g + 1) * rows, :HEAD] = q_ref[:, g * HEAD : (g + 1) * HEAD]
        stacked[g * rows : (g + 1) * rows, HEAD:] = q_doc[...]
    scale = math.log2(math.e) / math.sqrt(HEAD)
    tiles = [(t, t + rows) for t in range(0, total_keys, rows)]
    causal = lax.broadcasted_iota(jnp.int32, (tall, rows), 0) % rows >= lax.broadcasted_iota(
        jnp.int32, (tall, rows), 1
    )

    def score(g, scores, peak):
        q = stacked[g * tall : (g + 1) * tall, :]
        most = None
        for a, b in tiles:
            s = lax.dot_general(
                q, keys[a:b, :], (((1,), (1,)), ((), ())), preferred_element_type=jnp.float32
            )
            if a == past_keys:
                s = jnp.where(causal, s, HIDDEN)
            scores[:, a:b] = s
            for lane in range(0, rows, HEAD):
                part = s[:, lane : lane + HEAD]
                most = part if most is None else jnp.maximum(most, part)
        peak[...] = jnp.broadcast_to(jnp.max(most, axis=1, keepdims=True), (tall, HEAD))

    def mix(g, scores, peak):
        most = jnp.concatenate([peak[...]] * (rows // HEAD), axis=1)
        mixed = None
        for a, b in tiles:
            w = jnp.exp2((scores[:, a:b] - most) * scale).astype(jnp.bfloat16)
            part = jnp.dot(w, values[a:b, :], preferred_element_type=jnp.float32)
            mixed = part if mixed is None else mixed + part
        out = (mixed[:, :HEAD] / mixed[:, HEAD:]).astype(jnp.bfloat16)
        for h in range(STACK):
            at = (g * STACK + h) * HEAD
            out_ref[:, at : at + HEAD] = out[h * rows : (h + 1) * rows]

    buffers = ((scores_a, peak_a), (scores_b, peak_b))
    stacks = GROUP // STACK
    score(0, *buffers[0])
    for g in range(stacks):
        if g + 1 < stacks:
            score(g + 1, *buffers[(g + 1) % 2])
        mix(g, *buffers[g % 2])


def attend(first, units, queries, own_keys, own_values, window, q_doc, k_doc, attended):
    rows, width = queries.shape
    halves = KV_HEADS // UNITS
    sources, _, pairs = window.shape[:3]
    per_half = sources // halves
    total_keys = per_half * pairs * 16 + rows
    tall = STACK * rows
    head = lambda i, c: (0, UNITS * i + first + c)
    whole = lambda i, c: (0, 0)
    in_specs = [
        pl.BlockSpec((rows, GROUP * HEAD), head),
        pl.BlockSpec((rows, HEAD), head),
        pl.BlockSpec((rows, HEAD), head),
        pl.BlockSpec((per_half, 1, pairs, 2, 16, HEAD), lambda i, c: (i, c, 0, 0, 0, 0)),
        pl.BlockSpec((rows, HEAD), whole),
        pl.BlockSpec((total_keys, HEAD), whole),
    ]
    operands = [queries, own_keys, own_values, window, q_doc, k_doc]
    aliases = {}
    if attended is not None:
        in_specs.append(pl.BlockSpec(memory_space=pl.ANY))
        operands.append(attended)
        aliases = {6: 0}
    done = halves * units * GROUP * rows * total_keys
    return pl.pallas_call(
        attend_kernel,
        out_shape=jax.ShapeDtypeStruct((rows, width), jnp.bfloat16),
        grid=(halves, units),
        in_specs=in_specs,
        out_specs=pl.BlockSpec((rows, GROUP * HEAD), head),
        scratch_shapes=[
            pltpu.VMEM((total_keys, 2 * HEAD), jnp.bfloat16),
            pltpu.VMEM((total_keys, 2 * HEAD), jnp.bfloat16),
            pltpu.VMEM((GROUP * rows, 2 * HEAD), jnp.bfloat16),
            pltpu.VMEM((tall, total_keys), jnp.float32),
            pltpu.VMEM((tall, total_keys), jnp.float32),
            pltpu.VMEM((tall, HEAD), jnp.float32),
            pltpu.VMEM((tall, HEAD), jnp.float32),
        ],
        input_output_aliases=aliases,
        compiler_params=pltpu.CompilerParams(vmem_limit_bytes=44 << 20),
        cost_estimate=pl.CostEstimate(
            flops=done * 2 * 4 * HEAD, bytes_accessed=units * 4 << 20, transcendentals=done
        ),
        name="attend",
    )(*operands)


def body(queries, rotated_key_rows, stored_value_rows, doc_lengths, block_order):
    rows = queries.shape[0]
    axes = ("context", "tensor")
    blocks = block_order.shape[0]
    thin = rows * KV_HEADS // (UNITS * blocks)
    past = 8
    pieces = cut_pieces(rotated_key_rows, stored_value_rows, blocks)
    recv = lax.all_to_all(pieces, axes, split_axis=0, concat_axis=0, tiled=True)

    me = lax.axis_index("context") * lax.axis_size("tensor") + lax.axis_index("tensor")
    place = block_order[me]
    ends = jnp.cumsum(doc_lengths)
    far = jnp.full((HEAD - DOCS,), 1 << 30, jnp.int32)
    end = jnp.concatenate([ends, far])[None, :]
    start = jnp.concatenate([ends - doc_lengths, far])[None, :]
    q_pos = (place * rows + jnp.arange(rows, dtype=jnp.int32))[:, None]
    q_doc = ((q_pos >= start) & (q_pos < end)).astype(jnp.bfloat16)
    key = jnp.arange(past * rows, dtype=jnp.int32)
    within = key % 16
    slot = 2 * (key // 16 % (past // 2)) + within // thin
    key_block = place - 1 - slot
    key_pos = key_block * rows + key // (16 * (past // 2)) * thin + within % thin
    key_pos = jnp.concatenate([jnp.where(key_block >= 0, key_pos, -1)[:, None], q_pos])
    k_doc = jnp.where((key_pos >= start) & (key_pos < end), 0.0, HIDDEN).astype(jnp.bfloat16)

    attended = None
    for first, units in CHUNKS:
        sends = gather_windows(first, units, past, block_order, recv)
        window = lax.all_to_all(sends, axes, split_axis=0, concat_axis=0, tiled=True)
        attended = attend(
            first, units, queries, rotated_key_rows, stored_value_rows, window, q_doc, k_doc, attended
        )
    return attended


def solution(mesh):
    rows = P(("dp", "context", "tensor"), None)
    return jax.shard_map(
        body,
        mesh=mesh,
        in_specs=(rows, rows, rows, P("dp"), P("dp")),
        out_specs=rows,
        check_vma=False,
    )
```

time: 260 us -> 191 us (0.73)
  Pallas kernels: 126 us -> 56.7 us
  starting transfers between devices: 21.9 us -> 14.9 us
  waiting for transfers between devices: 67.6 us -> 73.7 us
  local copies, waits for them, and re-layouts: 9.29 us -> 11.9 us
    pallas_call x4 -> x2, Pallas kernels: 110 us -> 49.2 us  [attend(): pl.pallas_call(attend_kernel, out_shape=jax.ShapeDtypeStruct((rows, width...]
    pallas_call x4 -> x2, Pallas kernels: 15.5 us -> 7.27 us  [gather_windows(): pl.pallas_call(functools.partial(gather_kernel, past), out_shape=jax.Shap...]
    all_to_all x4 -> x2, starting transfers between devices: 21.9 us -> 14.9 us  [body(): lax.all_to_all(sends, axes, split_axis=0, concat_axis=0, tiled=True)]
    all_to_all x4 -> x2, waiting for transfers between devices: 67.6 us -> 73.7 us  [body(): lax.all_to_all(sends, axes, split_axis=0, concat_axis=0, tiled=True)]
    unnamed x18 -> x20, local copies, waits for them, and re-layouts: 6.47 us -> 11.2 us
  transfers between devices with their start and end apart: 4 -> 2, of which waited for: 3 -> 1; matrix products, arithmetic and copies ran while one was open for 1% -> 1% of each run, Pallas kernels for 36% -> 21%
where the time goes in v2:
time: 191 us; the launch traced here: 190 us
  waiting for transfers between devices  73.7 us (39%)
  Pallas kernels  56.7 us (30%)
  blocking collectives  30.1 us (16%)
  starting transfers between devices  14.9 us (8%)
  local copies, waits for them, and re-layouts  11.9 us (6%)
    all_to_all x2, waiting for transfers between devices, body(): lax.all_to_all(sends, axes, split_axis=0, concat_axis=0, tiled=True)  73.7 us
    pallas_call x2, Pallas kernels, attend(): pl.pallas_call(attend_kernel, out_shape=jax.ShapeDtypeStruct((rows, width...  49.2 us
    all_to_all x1, blocking collectives, body(): recv = lax.all_to_all(pieces, axes, split_axis=0, concat_axis=0, tiled=True)  30.1 us
    all_to_all x2, starting transfers between devices, body(): lax.all_to_all(sends, axes, split_axis=0, concat_axis=0, tiled=True)  14.9 us
    unnamed x20, local copies, waits for them, and re-layouts  11.2 us
    pallas_call x2, Pallas kernels, gather_windows(): pl.pallas_call(functools.partial(gather_kernel, past), out_shape=jax.Shap...  7.27 us
  transfers between devices with their start and end apart: 2, of which 1 were waited for; matrix products, arithmetic and copies ran while one was open for 1% of the time, Pallas kernels for 21%

profile of v2, /device:TPU:0, one launch (start us, length us, event | category | flops | bytes accessed | tf_op | source)
XLA Modules:
  0.0 190.1 jit_solution(7232595137091391224)
XLA Ops:
  0.0 1.0 copy-done.1
  1.0 1.0 copy-done.3
  2.1 0.2 cut_pieces.1
  2.3 30.1 %all_to_all.15.recv_ref = bf16[64,4,16,128]{3,2,1,0:T(8,128)(2,1)S(1)} all-to-all(bf16[64,4,16,128]{3,2,1,0:T(8,128)(2,1)S(1)} %cut_pieces.1), channel_id=1, replica_groups=mesh['dp'=2,'context'=8,'tensor'=8] {'context','tensor'}, dimensions={0} | all-to-all | bytes 2097152 | tf_op jit(solution)/shard_map/all_to_all | solution.py:208
  32.4 4.2 %gather_windows.3 = bf16[64,3,4,2,16,128]{5,4,3,2,1,0:T(8,128)(2,1)S(1)} custom-call(s32[64]{0:T(128)S(1)} %copy-done.6, bf16[64,4,16,128]{3,2,1,0:T(8,128)(2,1)S(1)} %all_to_all.15.recv_ref), custom_call_target="tpu_custom_call" | custom-call | bytes 6291456 | tf_op jit(solution)/shard_map/gather_windows/pallas_call | solution.py:78
  36.7 2.6 %copy-done = bf16[64,3,4,2,16,128]{5,4,3,2,1,0:T(8,128)(2,1)} copy-done((bf16[64,3,4,2,16,128]{5,4,3,2,1,0:T(8,128)(2,1)}, bf16[64,3,4,2,16,128]{5,4,3,2,1,0:T(8,128)(2,1)S(1)}, u32[]{:S(2)}) %copy-start) | copy-done | bytes 6291480
  39.3 5.8 %all-to-all-start.2 = ((bf16[64,3,4,2,16,128]{5,4,3,2,1,0:T(8,128)(2,1)}), bf16[64,3,4,2,16,128]{5,4,3,2,1,0:T(8,128)(2,1)}, u32[]{:S(2)}, u32[]{:S(2)}) async-start(bf16[64,3,4,2,16,128]{5,4,3,2,1,0:T(8,128)(2,1)} %copy-done), calls=%async_computation.2 | async-start | bytes 12582912 | tf_op jit(solution)/shard_map/all_to_all | solution.py:229
  45.2 0.6 dynamic_slice.3
  47.1 0.1 copy.8
  47.2 0.1 reduce
  47.4 0.1 compare_select_fusion.2
  47.5 0.1 and_convert_fusion.q_doc
  47.6 1.1 select_convert_fusion.k_doc
  48.7 3.0 %gather_windows.2 = bf16[64,1,4,2,16,128]{5,4,3,2,1,0:T(8,128)(2,1)} custom-call(s32[64]{0:T(128)S(1)} %copy-done.6, bf16[64,4,16,128]{3,2,1,0:T(8,128)(2,1)S(1)} %all_to_all.15.recv_ref), custom_call_target="tpu_custom_call" | custom-call | bytes 2097152 | tf_op jit(solution)/shard_map/gather_windows/pallas_call | solution.py:78
  51.7 73.7 %all-to-all-done.2.window = bf16[64,3,4,2,16,128]{5,4,3,2,1,0:T(8,128)(2,1)} async-done(((bf16[64,3,4,2,16,128]{5,4,3,2,1,0:T(8,128)(2,1)}), bf16[64,3,4,2,16,128]{5,4,3,2,1,0:T(8,128)(2,1)}, u32[]{:S(2)}, u32[]{:S(2)}) %all-to-all-start.2) | async-done | bytes 6291488 | tf_op jit(solution)/shard_map/all_to_all | solution.py:229
  125.4 9.1 %all-to-all-start.1 = ((bf16[64,1,4,2,16,128]{5,4,3,2,1,0:T(8,128)(2,1)}), bf16[64,1,4,2,16,128]{5,4,3,2,1,0:T(8,128)(2,1)S(1)}, u32[]{:S(2)}, u32[]{:S(2)}) async-start(bf16[64,1,4,2,16,128]{5,4,3,2,1,0:T(8,128)(2,1)} %gather_windows.2), calls=%async_computation.1 | async-start | bytes 4194304 | tf_op jit(solution)/shard_map/all_to_all | solution.py:229
  134.5 0.0 copy-start.4
  134.5 1.0 copy-done.4
  135.5 2.2 %copy-done.7 = bf16[256,8192]{1,0:T(8,128)(2,1)S(1)} copy-done((bf16[256,8192]{1,0:T(8,128)(2,1)S(1)}, bf16[256,8192]{1,0:T(8,128)(2,1)}, u32[]{:S(2)}) %copy-start.7) | copy-done | bytes 4194328
  137.7 36.8 %attend.2.rest_0_ = bf16[256,8192]{1,0:T(8,128)(2,1)} custom-call(bf16[256,8192]{1,0:T(8,128)(2,1)S(1)} %copy-done.7, bf16[256,1024]{1,0:T(8,128)(2,1)S(1)} %copy-done.2, bf16[256,1024]{1,0:T(8,128)(2,1)S(1)} %copy-done.4, bf16[64,3,4,2,16,128]{5,4,3,2,1,0:T(8,128)(2,1)} %all-to-all-done.2.window, bf16[256,128]{1,0:T(8,128)(2,1)S(1)} %and_convert_fusion.q_doc, ...), custom_call_target="tpu_custom_call" | custom-call | flops 28991029248 | bytes 12582912 | tf_op jit(solution)/shard_map/attend/pallas_call | solution.py:177
  174.5 0.0 all-to-all-done.1.window
  174.6 1.0 copy-done.5
  175.6 2.2 %copy-done.8 = bf16[256,8192]{1,0:T(8,128)(2,1)S(1)} copy-done((bf16[256,8192]{1,0:T(8,128)(2,1)S(1)}, bf16[256,8192]{1,0:T(8,128)(2,1)}, u32[]{:S(2)}) %copy-start.8) | copy-done | bytes 4194328
  177.8 12.4 %attend.3 = bf16[256,8192]{1,0:T(8,128)(2,1)} custom-call(bf16[256,8192]{1,0:T(8,128)(2,1)S(1)} %copy-done.8, bf16[256,1024]{1,0:T(8,128)(2,1)S(1)} %copy-done.2, bf16[256,1024]{1,0:T(8,128)(2,1)S(1)} %copy-done.5, bf16[64,1,4,2,16,128]{5,4,3,2,1,0:T(8,128)(2,1)S(1)} %all-to-all-done.1.window, ...), custom_call_target="tpu_custom_call", output_to_operand_aliasing={{}: (6, {})} | custom-call | flops 9663676416 | bytes 4194304 | tf_op jit(solution)/shard_map/attend/pallas_call | solution.py:177
  (19 shorter events, 0.1 us)
Async XLA Ops:
  0.0 1.0 copy-start.1
  1.0 1.0 copy-start.3
  2.1 30.4 %copy-start.6 = (s32[64]{0:T(128)S(1)}, s32[64]{0:T(128)}, u32[]{:S(2)}) copy-start(s32[64]{0:T(128)} %order_ref.3) | copy-start | bytes 772
  36.7 2.6 %copy-start = (bf16[64,3,4,2,16,128]{5,4,3,2,1,0:T(8,128)(2,1)}, bf16[64,3,4,2,16,128]{5,4,3,2,1,0:T(8,128)(2,1)S(1)}, u32[]{:S(2)}) copy-start(bf16[64,3,4,2,16,128]{5,4,3,2,1,0:T(8,128)(2,1)S(1)} %gather_windows.3) | copy-start | bytes 18874372
  39.3 7.7 %copy-start.9 = (s32[16]{0:T(128)S(1)}, s32[16]{0:T(128)}, u32[]{:S(2)}) copy-start(s32[16]{0:T(128)} %param.8) | copy-start | bytes 196
  39.3 86.1 %all-to-all-start.2 = ((bf16[64,3,4,2,16,128]{5,4,3,2,1,0:T(8,128)(2,1)}), bf16[64,3,4,2,16,128]{5,4,3,2,1,0:T(8,128)(2,1)}, u32[]{:S(2)}, u32[]{:S(2)}) async-start(bf16[64,3,4,2,16,128]{5,4,3,2,1,0:T(8,128)(2,1)} %copy-done), calls=%async_computation.2 | async-start | bytes 12582912 | tf_op jit(solution)/shard_map/all_to_all | solution.py:229
  51.7 82.8 %copy-start.2 = (bf16[256,1024]{1,0:T(8,128)(2,1)S(1)}, bf16[256,1024]{1,0:T(8,128)(2,1)}, u32[]{:S(2)}) copy-start(bf16[256,1024]{1,0:T(8,128)(2,1)} %k_own.3) | copy-start | bytes 1572868
  125.4 49.1 %all-to-all-start.1 = ((bf16[64,1,4,2,16,128]{5,4,3,2,1,0:T(8,128)(2,1)}), bf16[64,1,4,2,16,128]{5,4,3,2,1,0:T(8,128)(2,1)S(1)}, u32[]{:S(2)}, u32[]{:S(2)}) async-start(bf16[64,1,4,2,16,128]{5,4,3,2,1,0:T(8,128)(2,1)} %gather_windows.2), calls=%async_computation.1 | async-start | bytes 4194304 | tf_op jit(solution)/shard_map/all_to_all | solution.py:229
  134.5 1.0 copy-start.4
  135.5 2.2 %copy-start.7 = (bf16[256,8192]{1,0:T(8,128)(2,1)S(1)}, bf16[256,8192]{1,0:T(8,128)(2,1)}, u32[]{:S(2)}) copy-start(bf16[256,8192]{1,0:T(8,128)(2,1)} %q_ref.3) | copy-start | bytes 12582916
  174.5 1.0 copy-start.5
  175.6 2.2 %copy-start.8 = (bf16[256,8192]{1,0:T(8,128)(2,1)S(1)}, bf16[256,8192]{1,0:T(8,128)(2,1)}, u32[]{:S(2)}) copy-start(bf16[256,8192]{1,0:T(8,128)(2,1)} %q_ref.3) | copy-start | bytes 12582916

commit v3 on v2

--- a/solution.py
+++ b/solution.py
@@ -16,6 +16,7 @@
 UNITS = 4
 CHUNKS = ((0, 3), (3, 1))
 STACK = 4
+VMEM = 60 << 20
 
 
 def pieces_kernel(k_ref, v_ref, out_ref):
@@ -43,52 +44,63 @@
     return pl.pallas_call(
         pieces_kernel,
         out_shape=jax.ShapeDtypeStruct((blocks, UNITS, 2 * thin, HEAD), jnp.bfloat16),
-        compiler_params=pltpu.CompilerParams(vmem_limit_bytes=24 << 20),
+        compiler_params=pltpu.CompilerParams(vmem_limit_bytes=VMEM),
         cost_estimate=pl.CostEstimate(flops=0, bytes_accessed=2 << 20, transcendentals=0),
         name="cut_pieces",
     )(own_keys, own_values)
 
 
-def gather_kernel(past, order_ref, recv_ref, out_ref, inverse):
+def gather_kernel(past, order_ref, recv_ref, *rest):
+    out_refs, inverse = rest[:-1], rest[-1]
     blocks = order_ref.shape[0]
-    together = 4
-
-    @pl.when(pl.program_id(0) == 0)
+    part = out_refs[0].shape[0]
+    step = pl.program_id(0)
+
+    @pl.when(step == 0)
     def _():
         for j in range(blocks):
             inverse[order_ref[j]] = j
 
-    def fill(i, carry):
-        for d in range(together):
-            d = i * together + d
-            s = order_ref[d]
-            for u in range(past // 2):
-                a = recv_ref[inverse[jnp.maximum(s - 1 - 2 * u, 0)], 0].astype(jnp.float32)
-                b = recv_ref[inverse[jnp.maximum(s - 2 - 2 * u, 0)], 0].astype(jnp.float32)
-                out_ref[d, 0, u, 0] = jnp.concatenate([a[:8], b[:8]], axis=0).astype(jnp.bfloat16)
-                out_ref[d, 0, u, 1] = jnp.concatenate([a[8:], b[8:]], axis=0).astype(jnp.bfloat16)
+    def fill(d, carry):
+        s = order_ref[step * part + d]
+        for u in range(past // 2):
+            near = inverse[jnp.maximum(s - 1 - 2 * u, 0)]
+            far = inverse[jnp.maximum(s - 2 - 2 * u, 0)]
+            for (first, units), out_ref in zip(CHUNKS, out_refs):
+                for c in range(units):
+                    a = recv_ref[near, first + c].astype(jnp.float32)
+                    b = recv_ref[far, first + c].astype(jnp.float32)
+                    keys = jnp.concatenate([a[:8], b[:8]], axis=0)
+                    values = jnp.concatenate([a[8:], b[8:]], axis=0)
+                    out_ref[d, c, u, 0] = keys.astype(jnp.bfloat16)
+                    out_ref[d, c, u, 1] = values.astype(jnp.bfloat16)
         return carry
 
-    lax.fori_loop(0, blocks // together, fill, 0)
-
-
-def gather_windows(first, units, past, block_order, recv):
+    lax.fori_loop(0, part, fill, 0)
+
+
+def gather_windows(past, block_order, recv):
     blocks = block_order.shape[0]
     pairs = past // 2
+    part = blocks // 4
+    shape = lambda rows, units: (rows, units, pairs, 2, 16, HEAD)
     return pl.pallas_call(
         functools.partial(gather_kernel, past),
-        out_shape=jax.ShapeDtypeStruct((blocks, units, pairs, 2, 16, HEAD), jnp.bfloat16),
+        out_shape=[
+            jax.ShapeDtypeStruct(shape(blocks, units), jnp.bfloat16) for _, units in CHUNKS
+        ],
         grid_spec=pltpu.PrefetchScalarGridSpec(
             num_scalar_prefetch=1,
-            grid=(units,),
-            in_specs=[pl.BlockSpec((blocks, 1, 16, HEAD), lambda i, o: (0, first + i, 0, 0))],
-            out_specs=pl.BlockSpec(
-                (blocks, 1, pairs, 2, 16, HEAD), lambda i, o: (0, i, 0, 0, 0, 0)
-            ),
+            grid=(blocks // part,),
+            in_specs=[pl.BlockSpec((blocks, UNITS, 16, HEAD), lambda i, o: (0, 0, 0, 0))],
+            out_specs=[
+                pl.BlockSpec(shape(part, units), lambda i, o: (i, 0, 0, 0, 0, 0))
+                for _, units in CHUNKS
+            ],
             scratch_shapes=[pltpu.SMEM((blocks,), jnp.int32)],
         ),
-        compiler_params=pltpu.CompilerParams(vmem_limit_bytes=24 << 20),
-        cost_estimate=pl.CostEstimate(flops=0, bytes_accessed=units << 21, transcendentals=0),
+        compiler_params=pltpu.CompilerParams(vmem_limit_bytes=VMEM),
+        cost_estimate=pl.CostEstimate(flops=0, bytes_accessed=10 << 20, transcendentals=0),
         name="gather_windows",
     )(block_order, recv)
 
@@ -190,7 +202,7 @@
             pltpu.VMEM((tall, HEAD), jnp.float32),
         ],
         input_output_aliases=aliases,
-        compiler_params=pltpu.CompilerParams(vmem_limit_bytes=44 << 20),
+        compiler_params=pltpu.CompilerParams(vmem_limit_bytes=VMEM),
         cost_estimate=pl.CostEstimate(
             flops=done * 2 * 4 * HEAD, bytes_accessed=units * 4 << 20, transcendentals=done
         ),
@@ -206,6 +218,15 @@
     past = 8
     pieces = cut_pieces(rotated_key_rows, stored_value_rows, blocks)
     recv = lax.all_to_all(pieces, axes, split_axis=0, concat_axis=0, tiled=True)
+
+    sends = gather_windows(past, block_order, recv)
+    sends, own = lax.optimization_barrier((sends, (rotated_key_rows, stored_value_rows)))
+    windows = [lax.all_to_all(sends[0], axes, split_axis=0, concat_axis=0, tiled=True)]
+    windows[0], doc_lengths, block_order, rest = lax.optimization_barrier(
+        (windows[0], doc_lengths, block_order, sends[1:])
+    )
+    for send in rest:
+        windows.append(lax.all_to_all(send, axes, split_axis=0, concat_axis=0, tiled=True))
 
     me = lax.axis_index("context") * lax.axis_size("tensor") + lax.axis_index("tensor")
     place = block_order[me]
@@ -224,12 +245,8 @@
     k_doc = jnp.where((key_pos >= start) & (key_pos < end), 0.0, HIDDEN).astype(jnp.bfloat16)
 
     attended = None
-    for first, units in CHUNKS:
-        sends = gather_windows(first, units, past, block_order, recv)
-        window = lax.all_to_all(sends, axes, split_axis=0, concat_axis=0, tiled=True)
-        attended = attend(
-            first, units, queries, rotated_key_rows, stored_value_rows, window, q_doc, k_doc, attended
-        )
+    for (first, units), window in zip(CHUNKS, windows):
+        attended = attend(first, units, queries, *own, window, q_doc, k_doc, attended)
     return attended
 
 

time: 191 us -> 192 us (level)
  local copies, waits for them, and re-layouts: 11.9 us -> 2.03 us
  waiting for transfers between devices: 73.7 us -> 80.2 us
  Pallas kernels: 56.7 us -> 59.6 us
    unnamed x20 -> x6, local copies, waits for them, and re-layouts: 11.2 us -> 1.36 us
    all_to_all x2, waiting for transfers between devices: 73.7 us -> 80.2 us  [the longest x1 80.2 us: body(): lax.all_to_all(sends[0], axes, split_axis=0, concat_axis=0, tiled=True)]
    pallas_call x1, Pallas kernels: 0.25 us -> 2.41 us  [cut_pieces(): pl.pallas_call(pieces_kernel, out_shape=jax.ShapeDtypeStruct((blocks, UNI...]
    pallas_call x2 -> x1, Pallas kernels: 7.27 us -> 6.55 us  [gather_windows(): pl.pallas_call(functools.partial(gather_kernel, past), out_shape=[jax.Sha...]
  transfers between devices with their start and end apart: 2 -> 2, of which waited for: 1 -> 1; matrix products, arithmetic and copies ran while one was open for 1% -> 0% of each run, Pallas kernels for 21% -> 19%
where the time goes in v3:
time: 192 us; the launch traced here: 191 us
  waiting for transfers between devices  80.2 us (42%)
  Pallas kernels  59.6 us (31%)
  blocking collectives  30.4 us (16%)
  starting transfers between devices  14.9 us (8%)
  other arithmetic  2.79 us (1%)
  local copies, waits for them, and re-layouts  2.03 us (1%)
    all_to_all x1, waiting for transfers between devices, body(): lax.all_to_all(sends[0], axes, split_axis=0, concat_axis=0, tiled=True)  80.2 us
    pallas_call x2, Pallas kernels, attend(): pl.pallas_call(attend_kernel, out_shape=jax.ShapeDtypeStruct((rows, width...  50.7 us
    all_to_all x1, blocking collectives, body(): recv = lax.all_to_all(pieces, axes, split_axis=0, concat_axis=0, tiled=True)  30.4 us
    all_to_all x1, starting transfers between devices, body(): lax.all_to_all(send, axes, split_axis=0, concat_axis=0, tiled=True)  9.06 us
    pallas_call x1, Pallas kernels, gather_windows(): pl.pallas_call(functools.partial(gather_kernel, past), out_shape=[jax.Sha...  6.55 us
    all_to_all x1, starting transfers between devices, body(): lax.all_to_all(sends[0], axes, split_axis=0, concat_axis=0, tiled=True)  5.82 us
  transfers between devices with their start and end apart: 2, of which 1 were waited for; matrix products, arithmetic and copies ran while one was open for 0% of the time, Pallas kernels for 19%

profile of v3, /device:TPU:0, one launch (start us, length us, event | category | flops | bytes accessed | tf_op | source)
XLA Modules:
  0.0 191.4 jit_solution(7269192523503770070)
XLA Ops:
  0.0 2.4 %cut_pieces.1 = bf16[64,4,16,128]{3,2,1,0:T(8,128)(2,1)} custom-call(bf16[256,1024]{1,0:T(8,128)(2,1)} %k_own.1, bf16[256,1024]{1,0:T(8,128)(2,1)} %v_own.1), custom_call_target="tpu_custom_call" | custom-call | bytes 2097152 | tf_op jit(solution)/shard_map/cut_pieces/pallas_call | solution.py:44
  2.4 30.4 %all_to_all.15.recv_ref = bf16[64,4,16,128]{3,2,1,0:T(8,128)(2,1)} all-to-all(bf16[64,4,16,128]{3,2,1,0:T(8,128)(2,1)} %cut_pieces.1), channel_id=1, replica_groups=mesh['dp'=2,'context'=8,'tensor'=8] {'context','tensor'}, dimensions={0} | all-to-all | bytes 2097152 | tf_op jit(solution)/shard_map/all_to_all | solution.py:220
  32.8 6.5 %gather_windows.1 = (bf16[64,3,4,2,16,128]{5,4,3,2,1,0:T(8,128)(2,1)}, bf16[64,1,4,2,16,128]{5,4,3,2,1,0:T(8,128)(2,1)}) custom-call(s32[64]{0:T(128)} %order_ref.1, bf16[64,4,16,128]{3,2,1,0:T(8,128)(2,1)} %all_to_all.15.recv_ref), custom_call_target="tpu_custom_call" | custom-call | bytes 10485760 | tf_op jit(solution)/shard_map/gather_windows/pallas_call | solution.py:87
  39.4 0.0 copy-start.1
  39.4 0.0 copy-start.2
  39.4 5.8 %all-to-all-start.1 = ((bf16[64,3,4,2,16,128]{5,4,3,2,1,0:T(8,128)(2,1)}), bf16[64,3,4,2,16,128]{5,4,3,2,1,0:T(8,128)(2,1)}, u32[]{:S(2)}, u32[]{:S(2)}) async-start(bf16[64,3,4,2,16,128]{5,4,3,2,1,0:T(8,128)(2,1)} %get-tuple-element.19), calls=%async_computation.1 | async-start | bytes 12582912 | tf_op jit(solution)/shard_map/all_to_all | solution.py:224
  45.2 80.2 %all-to-all-done.1.window = bf16[64,3,4,2,16,128]{5,4,3,2,1,0:T(8,128)(2,1)} async-done(((bf16[64,3,4,2,16,128]{5,4,3,2,1,0:T(8,128)(2,1)}), bf16[64,3,4,2,16,128]{5,4,3,2,1,0:T(8,128)(2,1)}, u32[]{:S(2)}, u32[]{:S(2)}) %all-to-all-start.1) | async-done | bytes 6291488 | tf_op jit(solution)/shard_map/all_to_all | solution.py:224
  125.4 0.0 copy-done.1
  125.4 0.6 dynamic_slice.3
  127.4 0.1 compare_select_fusion.2
  127.4 0.0 copy-done.2
  127.4 0.1 copy.8
  127.6 0.1 reduce
  127.7 1.8 select_convert_fusion.k_doc
  129.5 0.7 and_convert_fusion.q_doc
  130.3 9.1 %all-to-all-start.2 = ((bf16[64,1,4,2,16,128]{5,4,3,2,1,0:T(8,128)(2,1)}), bf16[64,1,4,2,16,128]{5,4,3,2,1,0:T(8,128)(2,1)S(1)}, u32[]{:S(2)}, u32[]{:S(2)}) async-start(bf16[64,1,4,2,16,128]{5,4,3,2,1,0:T(8,128)(2,1)} %get-tuple-element.21), calls=%async_computation.2 | async-start | bytes 4194304 | tf_op jit(solution)/shard_map/all_to_all | solution.py:229
  139.3 36.8 %attend.2.rest_0_ = bf16[256,8192]{1,0:T(8,128)(2,1)} custom-call(bf16[256,8192]{1,0:T(8,128)(2,1)} %q_ref.3, bf16[256,1024]{1,0:T(8,128)(2,1)} %k_own.1, bf16[256,1024]{1,0:T(8,128)(2,1)} %v_own.1, bf16[64,3,4,2,16,128]{5,4,3,2,1,0:T(8,128)(2,1)} %all-to-all-done.1.window, bf16[256,128]{1,0:T(8,128)(2,1)} %and_convert_fusion.q_doc, ...), custom_call_target="tpu_custom_call" | custom-call | flops 28991029248 | bytes 12582912 | tf_op jit(solution)/shard_map/attend/pallas_call | solution.py:189
  176.1 0.0 all-to-all-done.2.window
  176.1 0.0 copy-start
  176.2 1.3 copy-done
  177.5 13.9 %attend.3 = bf16[256,8192]{1,0:T(8,128)(2,1)} custom-call(bf16[256,8192]{1,0:T(8,128)(2,1)} %q_ref.3, bf16[256,1024]{1,0:T(8,128)(2,1)} %k_own.1, bf16[256,1024]{1,0:T(8,128)(2,1)} %v_own.1, bf16[64,1,4,2,16,128]{5,4,3,2,1,0:T(8,128)(2,1)} %copy-done, bf16[256,128]{1,0:T(8,128)(2,1)} %and_convert_fusion.q_doc, ...), custom_call_target="tpu_custom_call", output_to_operand_aliasing={{}: (6, {})} | custom-call | flops 9663676416 | bytes 4194304 | tf_op jit(solution)/shard_map/attend/pallas_call | solution.py:189
  (7 shorter events, 0.1 us)
Async XLA Ops:
  39.4 86.1 %copy-start.1 = (s32[64]{0:T(128)S(1)}, s32[64]{0:T(128)}, u32[]{:S(2)}) copy-start(s32[64]{0:T(128)} %order_ref.1) | copy-start | bytes 772
  39.4 88.1 %copy-start.2 = (s32[16]{0:T(128)S(1)}, s32[16]{0:T(128)}, u32[]{:S(2)}) copy-start(s32[16]{0:T(128)} %param.8) | copy-start | bytes 196
  39.4 86.1 %all-to-all-start.1 = ((bf16[64,3,4,2,16,128]{5,4,3,2,1,0:T(8,128)(2,1)}), bf16[64,3,4,2,16,128]{5,4,3,2,1,0:T(8,128)(2,1)}, u32[]{:S(2)}, u32[]{:S(2)}) async-start(bf16[64,3,4,2,16,128]{5,4,3,2,1,0:T(8,128)(2,1)} %get-tuple-element.19), calls=%async_computation.1 | async-start | bytes 12582912 | tf_op jit(solution)/shard_map/all_to_all | solution.py:224
  130.3 45.9 %all-to-all-start.2 = ((bf16[64,1,4,2,16,128]{5,4,3,2,1,0:T(8,128)(2,1)}), bf16[64,1,4,2,16,128]{5,4,3,2,1,0:T(8,128)(2,1)S(1)}, u32[]{:S(2)}, u32[]{:S(2)}) async-start(bf16[64,1,4,2,16,128]{5,4,3,2,1,0:T(8,128)(2,1)} %get-tuple-element.21), calls=%async_computation.2 | async-start | bytes 4194304 | tf_op jit(solution)/shard_map/all_to_all | solution.py:229
  176.1 1.4 copy-start

commit v4 on v3

--- a/solution.py
+++ b/solution.py
@@ -11,12 +11,11 @@
 HEAD = 128
 GROUP = 8
 KV_HEADS = 8
-DOCS = 16
 HIDDEN = -1e30
 UNITS = 4
 CHUNKS = ((0, 3), (3, 1))
 STACK = 4
-VMEM = 60 << 20
+VMEM = 62 << 20
 
 
 def pieces_kernel(k_ref, v_ref, out_ref):
@@ -105,21 +104,67 @@
     )(block_order, recv)
 
 
-def attend_kernel(q_ref, k_own, v_own, window, q_doc, k_doc, *rest):
+def mark_documents(lengths_ref, place, keys, stacked):
+    total_keys, rows = keys.shape[0], stacked.shape[0] // GROUP
+    lane = lax.broadcasted_iota(jnp.int32, (8, HEAD), 1)
+    row = lax.broadcasted_iota(jnp.int32, (8, HEAD), 0)
+    start = jnp.full((8, HEAD), 1 << 30, jnp.int32)
+    end = start
+    at = 0
+    for d in range(lengths_ref.shape[0]):
+        start = jnp.where(lane == d, at, start)
+        at += lengths_ref[d]
+        end = jnp.where(lane == d, at, end)
+
+    def pair(base_a, base_b, inside, outside):
+        both = [
+            jnp.where((base + row >= start) & (base + row < end), inside, outside)
+            for base in (base_a, base_b)
+        ]
+        return jnp.concatenate(both, axis=0).astype(jnp.bfloat16)
+
+    past_keys = total_keys - rows
+    slots = past_keys // rows
+
+    def past(r, carry):
+        for u in range(slots // 2):
+            bases = []
+            for slot in (2 * u, 2 * u + 1):
+                block = place - 1 - slot
+                bases.append(jnp.where(block >= 0, block * rows + r * 8, -8))
+            to = pl.ds(pl.multiple_of((r * (slots // 2) + u) * 16, 16), 16)
+            keys[to, HEAD:] = pair(*bases, 0.0, HIDDEN)
+        return carry
+
+    lax.fori_loop(0, rows // 8, past, 0)
+    for r in range(rows // 16):
+        base = place * rows + r * 16
+        keys[past_keys + r * 16 : past_keys + r * 16 + 16, HEAD:] = pair(
+            base, base + 8, 0.0, HIDDEN
+        )
+        marks = pair(base, base + 8, 1.0, 0.0)
+        for g in range(GROUP):
+            stacked[g * rows + r * 16 : g * rows + r * 16 + 16, HEAD:] = marks
+
+
+def attend_kernel(lengths_ref, order_ref, me_ref, q_ref, k_own, v_own, window, *rest):
     out_ref, keys, values, stacked, scores_a, scores_b, peak_a, peak_b = rest[-8:]
     rows = q_ref.shape[0]
     total_keys = keys.shape[0]
     past_keys = total_keys - rows
     tall = STACK * rows
+
+    @pl.when((pl.program_id(0) == 0) & (pl.program_id(1) == 0))
+    def _():
+        mark_documents(lengths_ref, order_ref[me_ref[0]], keys, stacked)
+        values[:, HEAD:] = jnp.ones((total_keys, HEAD), jnp.bfloat16)
+
     keys[:past_keys, :HEAD] = window[:, 0, :, 0].reshape(past_keys, HEAD)
     keys[past_keys:, :HEAD] = k_own[...]
-    keys[:, HEAD:] = k_doc[...]
     values[:past_keys, :HEAD] = window[:, 0, :, 1].reshape(past_keys, HEAD)
     values[past_keys:, :HEAD] = v_own[...]
-    values[:, HEAD:] = jnp.ones((total_keys, HEAD), jnp.bfloat16)
     for g in range(GROUP):
         stacked[g * rows : (g + 1) * rows, :HEAD] = q_ref[:, g * HEAD : (g + 1) * HEAD]
-        stacked[g * rows : (g + 1) * rows, HEAD:] = q_doc[...]
     scale = math.log2(math.e) / math.sqrt(HEAD)
     tiles = [(t, t + rows) for t in range(0, total_keys, rows)]
     causal = lax.broadcasted_iota(jnp.int32, (tall, rows), 0) % rows >= lax.broadcasted_iota(
@@ -162,45 +207,45 @@
         mix(g, *buffers[g % 2])
 
 
-def attend(first, units, queries, own_keys, own_values, window, q_doc, k_doc, attended):
+def attend(first, units, lengths, order, me, queries, own_keys, own_values, window, attended):
     rows, width = queries.shape
     halves = KV_HEADS // UNITS
     sources, _, pairs = window.shape[:3]
     per_half = sources // halves
     total_keys = per_half * pairs * 16 + rows
     tall = STACK * rows
-    head = lambda i, c: (0, UNITS * i + first + c)
-    whole = lambda i, c: (0, 0)
+    head = lambda i, c, *scalars: (0, UNITS * i + first + c)
     in_specs = [
         pl.BlockSpec((rows, GROUP * HEAD), head),
         pl.BlockSpec((rows, HEAD), head),
         pl.BlockSpec((rows, HEAD), head),
-        pl.BlockSpec((per_half, 1, pairs, 2, 16, HEAD), lambda i, c: (i, c, 0, 0, 0, 0)),
-        pl.BlockSpec((rows, HEAD), whole),
-        pl.BlockSpec((total_keys, HEAD), whole),
+        pl.BlockSpec((per_half, 1, pairs, 2, 16, HEAD), lambda i, c, *scalars: (i, c, 0, 0, 0, 0)),
     ]
-    operands = [queries, own_keys, own_values, window, q_doc, k_doc]
+    operands = [lengths, order, me, queries, own_keys, own_values, window]
     aliases = {}
     if attended is not None:
         in_specs.append(pl.BlockSpec(memory_space=pl.ANY))
+        aliases = {len(operands): 0}
         operands.append(attended)
-        aliases = {6: 0}
     done = halves * units * GROUP * rows * total_keys
     return pl.pallas_call(
         attend_kernel,
         out_shape=jax.ShapeDtypeStruct((rows, width), jnp.bfloat16),
-        grid=(halves, units),
-        in_specs=in_specs,
-        out_specs=pl.BlockSpec((rows, GROUP * HEAD), head),
-        scratch_shapes=[
-            pltpu.VMEM((total_keys, 2 * HEAD), jnp.bfloat16),
-            pltpu.VMEM((total_keys, 2 * HEAD), jnp.bfloat16),
-            pltpu.VMEM((GROUP * rows, 2 * HEAD), jnp.bfloat16),
-            pltpu.VMEM((tall, total_keys), jnp.float32),
-            pltpu.VMEM((tall, total_keys), jnp.float32),
-            pltpu.VMEM((tall, HEAD), jnp.float32),
-            pltpu.VMEM((tall, HEAD), jnp.float32),
-        ],
+        grid_spec=pltpu.PrefetchScalarGridSpec(
+            num_scalar_prefetch=3,
+            grid=(halves, units),
+            in_specs=in_specs,
+            out_specs=pl.BlockSpec((rows, GROUP * HEAD), head),
+            scratch_shapes=[
+                pltpu.VMEM((total_keys, 2 * HEAD), jnp.bfloat16),
+                pltpu.VMEM((total_keys, 2 * HEAD), jnp.bfloat16),
+                pltpu.VMEM((GROUP * rows, 2 * HEAD), jnp.bfloat16),
+                pltpu.VMEM((tall, total_keys), jnp.float32),
+                pltpu.VMEM((tall, total_keys), jnp.float32),
+                pltpu.VMEM((tall, HEAD), jnp.float32),
+                pltpu.VMEM((tall, HEAD), jnp.float32),
+            ],
+        ),
         input_output_aliases=aliases,
         compiler_params=pltpu.CompilerParams(vmem_limit_bytes=VMEM),
         cost_estimate=pl.CostEstimate(
@@ -211,42 +256,25 @@
 
 
 def body(queries, rotated_key_rows, stored_value_rows, doc_lengths, block_order):
-    rows = queries.shape[0]
     axes = ("context", "tensor")
     blocks = block_order.shape[0]
-    thin = rows * KV_HEADS // (UNITS * blocks)
     past = 8
+    me = lax.axis_index("context") * lax.axis_size("tensor") + lax.axis_index("tensor")
+    me = me.astype(jnp.int32).reshape(1)
     pieces = cut_pieces(rotated_key_rows, stored_value_rows, blocks)
+    pieces, me = lax.optimization_barrier((pieces, me))
     recv = lax.all_to_all(pieces, axes, split_axis=0, concat_axis=0, tiled=True)
-
     sends = gather_windows(past, block_order, recv)
-    sends, own = lax.optimization_barrier((sends, (rotated_key_rows, stored_value_rows)))
-    windows = [lax.all_to_all(sends[0], axes, split_axis=0, concat_axis=0, tiled=True)]
-    windows[0], doc_lengths, block_order, rest = lax.optimization_barrier(
-        (windows[0], doc_lengths, block_order, sends[1:])
-    )
+    sends, me = lax.optimization_barrier((sends, me))
+    first = lax.all_to_all(sends[0], axes, split_axis=0, concat_axis=0, tiled=True)
+    first, me, rest = lax.optimization_barrier((first, me, sends[1:]))
+    windows = [first]
     for send in rest:
         windows.append(lax.all_to_all(send, axes, split_axis=0, concat_axis=0, tiled=True))
-
-    me = lax.axis_index("context") * lax.axis_size("tensor") + lax.axis_index("tensor")
-    place = block_order[me]
-    ends = jnp.cumsum(doc_lengths)
-    far = jnp.full((HEAD - DOCS,), 1 << 30, jnp.int32)
-    end = jnp.concatenate([ends, far])[None, :]
-    start = jnp.concatenate([ends - doc_lengths, far])[None, :]
-    q_pos = (place * rows + jnp.arange(rows, dtype=jnp.int32))[:, None]
-    q_doc = ((q_pos >= start) & (q_pos < end)).astype(jnp.bfloat16)
-    key = jnp.arange(past * rows, dtype=jnp.int32)
-    within = key % 16
-    slot = 2 * (key // 16 % (past // 2)) + within // thin
-    key_block = place - 1 - slot
-    key_pos = key_block * rows + key // (16 * (past // 2)) * thin + within % thin
-    key_pos = jnp.concatenate([jnp.where(key_block >= 0, key_pos, -1)[:, None], q_pos])
-    k_doc = jnp.where((key_pos >= start) & (key_pos < end), 0.0, HIDDEN).astype(jnp.bfloat16)
-
     attended = None
-    for (first, units), window in zip(CHUNKS, windows):
-        attended = attend(first, units, queries, *own, window, q_doc, k_doc, attended)
+    own = (queries, rotated_key_rows, stored_value_rows)
+    for (begin, units), window in zip(CHUNKS, windows):
+        attended = attend(begin, units, doc_lengths, block_order, me, *own, window, attended)
     return attended
 
 

time: 192 us -> 178 us (0.927)
  waiting for transfers between devices: 80.2 us -> 0.01 us
  blocking collectives: 30.4 us -> 110 us
  starting transfers between devices: 14.9 us -> 5.96 us
  other arithmetic: 2.79 us -> 0 us
  local copies, waits for them, and re-layouts: 2.03 us -> 0 us
    all_to_all x1 -> x0, waiting for transfers between devices: 80.2 us -> none  [body(): lax.all_to_all(sends[0], axes, split_axis=0, concat_axis=0, tiled=True)]
    all_to_all x0 -> x1, blocking collectives: none -> 79.4 us  [body(): lax.all_to_all(sends[0], axes, split_axis=0, concat_axis=0, tiled=True)]
    all_to_all x1 -> x0, starting transfers between devices: 5.82 us -> none  [body(): lax.all_to_all(sends[0], axes, split_axis=0, concat_axis=0, tiled=True)]
    all_to_all x1, starting transfers between devices: 9.06 us -> 5.96 us  [body(): lax.all_to_all(send, axes, split_axis=0, concat_axis=0, tiled=True)]
    convert_element_type x2 -> x0, other arithmetic: 2.52 us -> none  [the longest x1 1.8 us: body(): jnp.where((key_pos >= start) & (key_pos < end), 0.0, HIDDEN)]
  transfers between devices with their start and end apart: 2 -> 1, of which waited for: 1 -> 0; matrix products, arithmetic and copies ran while one was open for 0% -> 0% of each run, Pallas kernels for 19% -> 21%
where the time goes in v4:
time: 178 us; the launch traced here: 177 us
  blocking collectives  110 us (62%)
  Pallas kernels  61.1 us (34%)
  starting transfers between devices  5.96 us (3%)
    all_to_all x1, blocking collectives, body(): lax.all_to_all(sends[0], axes, split_axis=0, concat_axis=0, tiled=True)  79.4 us
    pallas_call x2, Pallas kernels, attend(): pl.pallas_call(attend_kernel, out_shape=jax.ShapeDtypeStruct((rows, width...  52.1 us
    all_to_all x1, blocking collectives, body(): recv = lax.all_to_all(pieces, axes, split_axis=0, concat_axis=0, tiled=True)  30.4 us
    pallas_call x1, Pallas kernels, gather_windows(): pl.pallas_call(functools.partial(gather_kernel, past), out_shape=[jax.Sha...  6.61 us
    all_to_all x1, starting transfers between devices, body(): lax.all_to_all(send, axes, split_axis=0, concat_axis=0, tiled=True)  5.96 us
  transfers between devices with their start and end apart: 1, of which 0 were waited for; matrix products, arithmetic and copies ran while one was open for 0% of the time, Pallas kernels for 21%

profile of v4, /device:TPU:0, one launch (start us, length us, event | category | flops | bytes accessed | tf_op | source)
XLA Modules:
  0.0 176.9 jit_solution(13469035297553719290)
XLA Ops:
  0.0 2.4 %cut_pieces.1 = bf16[64,4,16,128]{3,2,1,0:T(8,128)(2,1)} custom-call(bf16[256,1024]{1,0:T(8,128)(2,1)} %k_own.3, bf16[256,1024]{1,0:T(8,128)(2,1)} %v_own.3), custom_call_target="tpu_custom_call" | custom-call | bytes 2097152 | tf_op jit(solution)/shard_map/cut_pieces/pallas_call | solution.py:43
  2.4 30.4 %all_to_all.15.recv_ref = bf16[64,4,16,128]{3,2,1,0:T(8,128)(2,1)} all-to-all(bf16[64,4,16,128]{3,2,1,0:T(8,128)(2,1)} %cut_pieces.1), channel_id=1, replica_groups=mesh['dp'=2,'context'=8,'tensor'=8] {'context','tensor'}, dimensions={0} | all-to-all | bytes 2097152 | tf_op jit(solution)/shard_map/all_to_all | solution.py:266
  32.8 6.6 %gather_windows.1 = (bf16[64,3,4,2,16,128]{5,4,3,2,1,0:T(8,128)(2,1)}, bf16[64,1,4,2,16,128]{5,4,3,2,1,0:T(8,128)(2,1)}) custom-call(s32[64]{0:T(128)} %order_ref.5, bf16[64,4,16,128]{3,2,1,0:T(8,128)(2,1)} %all_to_all.15.recv_ref), custom_call_target="tpu_custom_call" | custom-call | bytes 10485760 | tf_op jit(solution)/shard_map/gather_windows/pallas_call | solution.py:86
  39.4 79.4 %all_to_all.16.window = bf16[64,3,4,2,16,128]{5,4,3,2,1,0:T(8,128)(2,1)} all-to-all(bf16[64,3,4,2,16,128]{5,4,3,2,1,0:T(8,128)(2,1)} %get-tuple-element.19), channel_id=1, replica_groups=mesh['dp'=2,'context'=8,'tensor'=8] {'context','tensor'}, dimensions={0} | all-to-all | bytes 12582912 | tf_op jit(solution)/shard_map/all_to_all | solution.py:269
  118.9 6.0 %all-to-all-start.2 = ((bf16[64,1,4,2,16,128]{5,4,3,2,1,0:T(8,128)(2,1)}), bf16[64,1,4,2,16,128]{5,4,3,2,1,0:T(8,128)(2,1)}, u32[]{:S(2)}, u32[]{:S(2)}) async-start(bf16[64,1,4,2,16,128]{5,4,3,2,1,0:T(8,128)(2,1)} %get-tuple-element.23), calls=%async_computation.2 | async-start | bytes 4194304 | tf_op jit(solution)/shard_map/all_to_all | solution.py:273
  124.8 37.2 %attend.2.rest_0_ = bf16[256,8192]{1,0:T(8,128)(2,1)} custom-call(s32[16]{0:T(128)} %lengths_ref.3, s32[64]{0:T(128)} %order_ref.5, s32[1]{0:T(128)} %bitcast.me_ref, bf16[256,8192]{1,0:T(8,128)(2,1)} %q_ref.3, bf16[256,1024]{1,0:T(8,128)(2,1)} %k_own.3, bf16[256,1024]{1,0:T(8,128)(2,1)} %v_own.3, bf16[64,3,4,2,16,128]{5,4,3,2,1,0:T(8,128)(2,1)} %all_to_all.16.window), custom_call_target="tpu_custom_call" | custom-call | flops 28991029248 | bytes 12582912 | tf_op jit(solution)/shard_map/attend/pallas_call | solution.py:231
  162.0 0.0 all-to-all-done.2.window
  162.0 14.9 %attend.3 = bf16[256,8192]{1,0:T(8,128)(2,1)} custom-call(s32[16]{0:T(128)} %lengths_ref.3, s32[64]{0:T(128)} %order_ref.5, s32[1]{0:T(128)} %bitcast.me_ref, bf16[256,8192]{1,0:T(8,128)(2,1)} %q_ref.3, bf16[256,1024]{1,0:T(8,128)(2,1)} %k_own.3, bf16[256,1024]{1,0:T(8,128)(2,1)} %v_own.3, ...), custom_call_target="tpu_custom_call", output_to_operand_aliasing={{}: (7, {})} | custom-call | flops 9663676416 | bytes 4194304 | tf_op jit(solution)/shard_map/attend/pallas_call | solution.py:231
Async XLA Ops:
  118.9 43.2 %all-to-all-start.2 = ((bf16[64,1,4,2,16,128]{5,4,3,2,1,0:T(8,128)(2,1)}), bf16[64,1,4,2,16,128]{5,4,3,2,1,0:T(8,128)(2,1)}, u32[]{:S(2)}, u32[]{:S(2)}) async-start(bf16[64,1,4,2,16,128]{5,4,3,2,1,0:T(8,128)(2,1)} %get-tuple-element.23), calls=%async_computation.2 | async-start | bytes 4194304 | tf_op jit(solution)/shard_map/all_to_all | solution.py:273

commit v5 on v4

v5 whole, which is shorter than its diff:
```python
import functools
import math

import jax
import jax.numpy as jnp
from jax import lax
from jax.experimental import pallas as pl
from jax.experimental.pallas import tpu as pltpu
from jax.sharding import PartitionSpec as P

HEAD = 128
GROUP = 8
KV_HEADS = 8
HIDDEN = -1e30
CHUNKS = ((0, 5), (5, 2), (7, 1))
THIN = 4
STACK = 4
VMEM = 62 << 20


def pieces_kernel(k_ref, v_ref, out_ref):
    tall = 16
    lower = lax.broadcasted_iota(jnp.int32, (8, HEAD), 0) < THIN

    def some_rows(r, carry):
        rows = pl.ds(pl.multiple_of(r * tall, tall), tall)
        for pair in range(KV_HEADS // 2):
            halves = []
            for h in (2 * pair, 2 * pair + 1):
                k = k_ref[rows, h * HEAD : (h + 1) * HEAD].astype(jnp.float32)
                v = v_ref[rows, h * HEAD : (h + 1) * HEAD].astype(jnp.float32)
                parts = []
                for at in (0, 8):
                    k8, v8 = k[at : at + 8], v[at : at + 8]
                    parts.append(jnp.where(lower, k8, pltpu.roll(v8, THIN, 0)))
                    parts.append(jnp.where(lower, pltpu.roll(k8, THIN, 0), v8))
                halves.append(parts)
            for j in range(tall // THIN):
                both = jnp.concatenate([halves[0][j], halves[1][j]], axis=0)
                out_ref[r * (tall // THIN) + j, pair] = both.astype(jnp.bfloat16)
        return carry

    lax.fori_loop(0, k_ref.shape[0] // tall, some_rows, 0, unroll=2)


def cut_pieces(own_keys, own_values):
    blocks = own_keys.shape[0] // THIN
    return pl.pallas_call(
        pieces_kernel,
        out_shape=jax.ShapeDtypeStruct((blocks, KV_HEADS // 2, 16, HEAD), jnp.bfloat16),
        compiler_params=pltpu.CompilerParams(vmem_limit_bytes=VMEM),
        cost_estimate=pl.CostEstimate(flops=0, bytes_accessed=2 << 20, transcendentals=0),
        name="cut_pieces",
    )(own_keys, own_values)


def gather_kernel(past, order_ref, recv_ref, *rest):
    out_refs, (inverse, plain, rolled) = rest[:-3], rest[-3:]
    blocks = order_ref.shape[0]
    part = out_refs[0].shape[0]
    step = pl.program_id(0)
    lower = lax.broadcasted_iota(jnp.int32, (8, HEAD), 0) < THIN

    @pl.when(step == 0)
    def _():
        for j in range(blocks):
            inverse[order_ref[j]] = j

        def open_block(j, carry):
            for pair in range(KV_HEADS // 2):
                x = recv_ref[j, pair].astype(jnp.float32)
                for half in range(2):
                    h = 2 * pair + half
                    x8 = x[8 * half : 8 * half + 8]
                    plain[j, h] = x8
                    rolled[j, h] = pltpu.roll(x8, THIN, 0)
            return carry

        lax.fori_loop(0, blocks, open_block, 0, unroll=4)

    def fill(d, carry):
        s = order_ref[step * part + d]
        held = [inverse[jnp.maximum(s - 1 - slot, 0)] for slot in range(past)]
        for (first, units), out_ref in zip(CHUNKS, out_refs):
            for c in range(units):
                h = first + c
                for tile in range(past // 4):
                    keys, values = [], []
                    for slot in (4 * tile, 4 * tile + 2):
                        near, far = held[slot], held[slot + 1]
                        keys.append(jnp.where(lower, plain[near, h], rolled[far, h]))
                        values.append(jnp.where(lower, rolled[near, h], plain[far, h]))
                    out_ref[d, c, 0, tile] = jnp.concatenate(keys, axis=0).astype(jnp.bfloat16)
                    out_ref[d, c, 1, tile] = jnp.concatenate(values, axis=0).astype(jnp.bfloat16)
        return carry

    lax.fori_loop(0, part, fill, 0, unroll=2)


def gather_windows(past, block_order, recv):
    blocks = block_order.shape[0]
    part = blocks // 4
    shape = lambda rows, units: (rows, units, 2, past // 4, 16, HEAD)
    return pl.pallas_call(
        functools.partial(gather_kernel, past),
        out_shape=[
            jax.ShapeDtypeStruct(shape(blocks, units), jnp.bfloat16) for _, units in CHUNKS
        ],
        grid_spec=pltpu.PrefetchScalarGridSpec(
            num_scalar_prefetch=1,
            grid=(blocks // part,),
            in_specs=[pl.BlockSpec((blocks, KV_HEADS // 2, 16, HEAD), lambda i, o: (0, 0, 0, 0))],
            out_specs=[
                pl.BlockSpec(shape(part, units), lambda i, o: (i, 0, 0, 0, 0, 0))
                for _, units in CHUNKS
            ],
            scratch_shapes=[
                pltpu.SMEM((blocks,), jnp.int32),
                pltpu.VMEM((blocks, KV_HEADS, 8, HEAD), jnp.float32),
                pltpu.VMEM((blocks, KV_HEADS, 8, HEAD), jnp.float32),
            ],
        ),
        compiler_params=pltpu.CompilerParams(vmem_limit_bytes=VMEM),
        cost_estimate=pl.CostEstimate(flops=0, bytes_accessed=10 << 20, transcendentals=0),
        name="gather_windows",
    )(block_order, recv)


def mark_documents(lengths_ref, place, keys, stacked):
    total_keys, rows = keys.shape[0], stacked.shape[0] // GROUP
    lane = lax.broadcasted_iota(jnp.int32, (8, HEAD), 1)
    row = lax.broadcasted_iota(jnp.int32, (8, HEAD), 0)
    start = jnp.full((8, HEAD), 1 << 30, jnp.int32)
    end = start
    at = 0
    for d in range(lengths_ref.shape[0]):
        start = jnp.where(lane == d, at, start)
        at += lengths_ref[d]
        end = jnp.where(lane == d, at, end)

    def pair(pos_a, pos_b, inside, outside):
        both = [
            jnp.where((pos >= start) & (pos < end), inside, outside) for pos in (pos_a, pos_b)
        ]
        return jnp.concatenate(both, axis=0).astype(jnp.bfloat16)

    past_keys = total_keys - rows
    slots = past_keys // rows
    origins = []
    for slot in range(0, slots, 2):
        block = place - 1 - slot - row // THIN
        origins.append(jnp.where(block >= 0, block * rows + row % THIN, -(1 << 20)))

    def past(i, carry):
        for tile in range(slots // 4):
            to = pl.ds(pl.multiple_of((i * (slots // 4) + tile) * 16, 16), 16)
            pos = [origins[2 * tile + half] + i * THIN for half in range(2)]
            keys[to, HEAD:] = pair(*pos, 0.0, HIDDEN)
        return carry

    lax.fori_loop(0, rows // THIN, past, 0, unroll=4)
    for r in range(0, rows, 16):
        base = place * rows + r + row
        keys[past_keys + r : past_keys + r + 16, HEAD:] = pair(base, base + 8, 0.0, HIDDEN)
        marks = pair(base, base + 8, 1.0, 0.0)
        for g in range(GROUP):
            stacked[g * rows + r : g * rows + r + 16, HEAD:] = marks


def attend_kernel(lengths_ref, order_ref, me_ref, q_ref, k_own, v_own, window, *rest):
    out_ref, keys, values, stacked, scores_a, scores_b, peak_a, peak_b = rest[-8:]
    rows = q_ref.shape[0]
    total_keys = keys.shape[0]
    past_keys = total_keys - rows
    tall = STACK * rows

    @pl.when(pl.program_id(0) == 0)
    def _():
        mark_documents(lengths_ref, order_ref[me_ref[0]], keys, stacked)
        values[:, HEAD:] = jnp.ones((total_keys, HEAD), jnp.bfloat16)

    keys[:past_keys, :HEAD] = window[:, 0, 0].reshape(past_keys, HEAD)
    keys[past_keys:, :HEAD] = k_own[...]
    values[:past_keys, :HEAD] = window[:, 0, 1].reshape(past_keys, HEAD)
    values[past_keys:, :HEAD] = v_own[...]
    for g in range(GROUP):
        stacked[g * rows : (g + 1) * rows, :HEAD] = q_ref[:, g * HEAD : (g + 1) * HEAD]
    scale = math.log2(math.e) / math.sqrt(HEAD)
    tiles = [(t, t + rows) for t in range(0, total_keys, rows)]
    causal = lax.broadcasted_iota(jnp.int32, (tall, rows), 0) % rows >= lax.broadcasted_iota(
        jnp.int32, (tall, rows), 1
    )

    def score(g, scores, peak):
        q = stacked[g * tall : (g + 1) * tall, :]
        most = None
        for a, b in tiles:
            s = lax.dot_general(
                q, keys[a:b, :], (((1,), (1,)), ((), ())), preferred_element_type=jnp.float32
            )
            if a == past_keys:
                s = jnp.where(causal, s, HIDDEN)
            scores[:, a:b] = s
            for lane in range(0, rows, HEAD):
                part = s[:, lane : lane + HEAD]
                most = part if most is None else jnp.maximum(most, part)
        peak[...] = jnp.broadcast_to(jnp.max(most, axis=1, keepdims=True), (tall, HEAD))

    def mix(g, scores, peak):
        most = jnp.concatenate([peak[...]] * (rows // HEAD), axis=1)
        mixed = None
        for a, b in tiles:
            w = jnp.exp2((scores[:, a:b] - most) * scale).astype(jnp.bfloat16)
            part = jnp.dot(w, values[a:b, :], preferred_element_type=jnp.float32)
            mixed = part if mixed is None else mixed + part
        out = (mixed[:, :HEAD] / mixed[:, HEAD:]).astype(jnp.bfloat16)
        for h in range(STACK):
            at = (g * STACK + h) * HEAD
            out_ref[:, at : at + HEAD] = out[h * rows : (h + 1) * rows]

    buffers = ((scores_a, peak_a), (scores_b, peak_b))
    stacks = GROUP // STACK
    score(0, *buffers[0])
    for g in range(stacks):
        if g + 1 < stacks:
            score(g + 1, *buffers[(g + 1) % 2])
        mix(g, *buffers[g % 2])


def attend(first, units, lengths, order, me, queries, own_keys, own_values, window, attended):
    rows, width = queries.shape
    sources, _, _, tiles = window.shape[:4]
    total_keys = sources * tiles * 16 + rows
    tall = STACK * rows
    head = lambda c, *scalars: (0, first + c)
    in_specs = [
        pl.BlockSpec((rows, GROUP * HEAD), head),
        pl.BlockSpec((rows, HEAD), head),
        pl.BlockSpec((rows, HEAD), head),
        pl.BlockSpec((sources, 1, 2, tiles, 16, HEAD), lambda c, *scalars: (0, c, 0, 0, 0, 0)),
    ]
    operands = [lengths, order, me, queries, own_keys, own_values, window]
    aliases = {}
    if attended is not None:
        in_specs.append(pl.BlockSpec(memory_space=pl.ANY))
        aliases = {len(operands): 0}
        operands.append(attended)
    done = units * GROUP * rows * total_keys
    return pl.pallas_call(
        attend_kernel,
        out_shape=jax.ShapeDtypeStruct((rows, width), jnp.bfloat16),
        grid_spec=pltpu.PrefetchScalarGridSpec(
            num_scalar_prefetch=3,
            grid=(units,),
            in_specs=in_specs,
            out_specs=pl.BlockSpec((rows, GROUP * HEAD), head),
            scratch_shapes=[
                pltpu.VMEM((total_keys, 2 * HEAD), jnp.bfloat16),
                pltpu.VMEM((total_keys, 2 * HEAD), jnp.bfloat16),
                pltpu.VMEM((GROUP * rows, 2 * HEAD), jnp.bfloat16),
                pltpu.VMEM((tall, total_keys), jnp.float32),
                pltpu.VMEM((tall, total_keys), jnp.float32),
                pltpu.VMEM((tall, HEAD), jnp.float32),
                pltpu.VMEM((tall, HEAD), jnp.float32),
            ],
        ),
        input_output_aliases=aliases,
        compiler_params=pltpu.CompilerParams(vmem_limit_bytes=VMEM),
        cost_estimate=pl.CostEstimate(
            flops=done * 2 * 4 * HEAD, bytes_accessed=units << 21, transcendentals=done
        ),
        name="attend",
    )(*operands)


def body(queries, rotated_key_rows, stored_value_rows, doc_lengths, block_order):
    axes = ("context", "tensor")
    past = 8
    me = lax.axis_index("context") * lax.axis_size("tensor") + lax.axis_index("tensor")
    me = me.astype(jnp.int32).reshape(1)
    pieces = cut_pieces(rotated_key_rows, stored_value_rows)
    pieces, me = lax.optimization_barrier((pieces, me))
    recv = lax.all_to_all(pieces, axes, split_axis=0, concat_axis=0, tiled=True)
    sends = gather_windows(past, block_order, recv)
    sends, me = lax.optimization_barrier((sends, me))
    window = lax.all_to_all(sends[0], axes, split_axis=0, concat_axis=0, tiled=True)
    window, me, sends = lax.optimization_barrier((window, me, sends))
    own = (queries, rotated_key_rows, stored_value_rows)
    attended = None
    for step, (first, units) in enumerate(CHUNKS):
        here = window
        if step + 1 < len(CHUNKS):
            send = sends[step + 1]
            if step:
                send, attended = lax.optimization_barrier((send, attended))
            window = lax.all_to_all(send, axes, split_axis=0, concat_axis=0, tiled=True)
        attended = attend(first, units, doc_lengths, block_order, me, *own, here, attended)
    return attended


def solution(mesh):
    rows = P(("dp", "context", "tensor"), None)
    return jax.shard_map(
        body,
        mesh=mesh,
        in_specs=(rows, rows, rows, P("dp"), P("dp")),
        out_specs=rows,
        check_vma=False,
    )
```

time: 178 us -> 183 us (1.028)
  blocking collectives: 110 us -> 98.8 us
  starting transfers between devices: 5.96 us -> 16 us
  waiting for transfers between devices: 0.01 us -> 2.79 us
  Pallas kernels: 61.1 us -> 63.7 us
    all_to_all x1, blocking collectives: 79.4 us -> 68.4 us  [body(): lax.all_to_all(sends[0], axes, split_axis=0, concat_axis=0, tiled=True)]
    all_to_all x1 -> x2, starting transfers between devices: 5.96 us -> 16 us  [body(): window = lax.all_to_all(send, axes, split_axis=0, concat_axis=0, tiled=True)]
    all_to_all x1 -> x2, waiting for transfers between devices: 0.01 us -> 2.79 us  [body(): window = lax.all_to_all(send, axes, split_axis=0, concat_axis=0, tiled=True)]
    pallas_call x2 -> x3, Pallas kernels: 52.1 us -> 54.7 us  [attend(): pl.pallas_call(attend_kernel, out_shape=jax.ShapeDtypeStruct((rows, width...]
  transfers between devices with their start and end apart: 1 -> 2, of which waited for: 0 -> 1; matrix products, arithmetic and copies ran while one was open for 0% -> 0% of each run, Pallas kernels for 21% -> 25%
where the time goes in v5:
time: 183 us; the launch traced here: 182 us
  blocking collectives  98.8 us (54%)
  Pallas kernels  63.7 us (35%)
  starting transfers between devices  16 us (9%)
  waiting for transfers between devices  2.79 us (2%)
    all_to_all x1, blocking collectives, body(): lax.all_to_all(sends[0], axes, split_axis=0, concat_axis=0, tiled=True)  68.4 us
    pallas_call x3, Pallas kernels, attend(): pl.pallas_call(attend_kernel, out_shape=jax.ShapeDtypeStruct((rows, width...  54.7 us
    all_to_all x1, blocking collectives, body(): recv = lax.all_to_all(pieces, axes, split_axis=0, concat_axis=0, tiled=True)  30.4 us
    all_to_all x2, starting transfers between devices, body(): window = lax.all_to_all(send, axes, split_axis=0, concat_axis=0, tiled=True)  16 us
    pallas_call x1, Pallas kernels, gather_windows(): pl.pallas_call(functools.partial(gather_kernel, past), out_shape=[jax.Sha...  6.65 us
  transfers between devices with their start and end apart: 2, of which 1 were waited for; matrix products, arithmetic and copies ran while one was open for 0% of the time, Pallas kernels for 25%

profile of v5, /device:TPU:0, one launch (start us, length us, event | category | flops | bytes accessed | tf_op | source)
XLA Modules:
  0.0 182.3 jit_solution(891494683073262687)
XLA Ops:
  0.0 2.4 %cut_pieces.1 = bf16[64,4,16,128]{3,2,1,0:T(8,128)(2,1)} custom-call(bf16[256,1024]{1,0:T(8,128)(2,1)} %k_own.5, bf16[256,1024]{1,0:T(8,128)(2,1)} %v_own.5), custom_call_target="tpu_custom_call" | custom-call | bytes 2097152 | tf_op jit(solution)/shard_map/cut_pieces/pallas_call | solution.py:48
  2.4 30.4 %all_to_all.20.recv_ref = bf16[64,4,16,128]{3,2,1,0:T(8,128)(2,1)} all-to-all(bf16[64,4,16,128]{3,2,1,0:T(8,128)(2,1)} %cut_pieces.1), channel_id=1, replica_groups=mesh['dp'=2,'context'=8,'tensor'=8] {'context','tensor'}, dimensions={0} | all-to-all | bytes 2097152 | tf_op jit(solution)/shard_map/all_to_all | solution.py:283
  32.8 6.7 %gather_windows.1 = (bf16[64,5,2,2,16,128]{5,4,3,2,1,0:T(8,128)(2,1)}, bf16[64,2,2,2,16,128]{5,4,3,2,1,0:T(8,128)(2,1)}, bf16[64,1,2,2,16,128]{5,4,3,2,1,0:T(8,128)(2,1)}) custom-call(s32[64]{0:T(128)} %order_ref.7, bf16[64,4,16,128]{3,2,1,0:T(8,128)(2,1)} %all_to_all.20.recv_ref), custom_call_target="tpu_custom_call" | custom-call | bytes 10485760 | tf_op jit(solution)/shard_map/gather_windows/pallas_call | solution.py:104
  39.5 68.4 %all_to_all.21.window = bf16[64,5,2,2,16,128]{5,4,3,2,1,0:T(8,128)(2,1)} all-to-all(bf16[64,5,2,2,16,128]{5,4,3,2,1,0:T(8,128)(2,1)} %get-tuple-element.25), channel_id=1, replica_groups=mesh['dp'=2,'context'=8,'tensor'=8] {'context','tensor'}, dimensions={0} | all-to-all | bytes 10485760 | tf_op jit(solution)/shard_map/all_to_all | solution.py:286
  107.9 5.6 %all-to-all-start.3 = ((bf16[64,2,2,2,16,128]{5,4,3,2,1,0:T(8,128)(2,1)}), bf16[64,2,2,2,16,128]{5,4,3,2,1,0:T(8,128)(2,1)}, u32[]{:S(2)}, u32[]{:S(2)}) async-start(bf16[64,2,2,2,16,128]{5,4,3,2,1,0:T(8,128)(2,1)} %get-tuple-element.33), calls=%async_computation.3 | async-start | bytes 4194304 | tf_op jit(solution)/shard_map/all_to_all | solution.py:296
  113.4 31.2 %attend.3.rest_0_ = bf16[256,8192]{1,0:T(8,128)(2,1)} custom-call(s32[16]{0:T(128)} %lengths_ref.5, s32[64]{0:T(128)} %order_ref.7, s32[1]{0:T(128)} %bitcast.me_ref, bf16[256,8192]{1,0:T(8,128)(2,1)} %q_ref.5, bf16[256,1024]{1,0:T(8,128)(2,1)} %k_own.5, bf16[256,1024]{1,0:T(8,128)(2,1)} %v_own.5, bf16[64,5,2,2,16,128]{5,4,3,2,1,0:T(8,128)(2,1)} %all_to_all.21.window), custom_call_target="tpu_custom_call" | custom-call | flops 24159191040 | bytes 10485760 | tf_op jit(solution)/shard_map/attend/pallas_call | solution.py:249
  144.6 0.0 all-to-all-done.3.window
  144.6 10.4 %all-to-all-start.2 = ((bf16[64,1,2,2,16,128]{5,4,3,2,1,0:T(8,128)(2,1)}), bf16[64,1,2,2,16,128]{5,4,3,2,1,0:T(8,128)(2,1)S(1)}, u32[]{:S(2)}, u32[]{:S(2)}) async-start(bf16[64,1,2,2,16,128]{5,4,3,2,1,0:T(8,128)(2,1)} %get-tuple-element.32), calls=%async_computation.2 | async-start | bytes 2097152 | tf_op jit(solution)/shard_map/all_to_all | solution.py:296
  155.1 14.5 %attend.4.rest_0_ = bf16[256,8192]{1,0:T(8,128)(2,1)} custom-call(s32[16]{0:T(128)} %lengths_ref.5, s32[64]{0:T(128)} %order_ref.7, s32[1]{0:T(128)} %bitcast.me_ref, bf16[256,8192]{1,0:T(8,128)(2,1)} %q_ref.5, bf16[256,1024]{1,0:T(8,128)(2,1)} %k_own.5, bf16[256,1024]{1,0:T(8,128)(2,1)} %v_own.5, ...), custom_call_target="tpu_custom_call", output_to_operand_aliasing={{}: (7, {})} | custom-call | flops 9663676416 | bytes 4194304 | tf_op jit(solution)/shard_map/attend/pallas_call | solution.py:249
  169.6 2.8 %all-to-all-done.2.window = bf16[64,1,2,2,16,128]{5,4,3,2,1,0:T(8,128)(2,1)S(1)} async-done(((bf16[64,1,2,2,16,128]{5,4,3,2,1,0:T(8,128)(2,1)}), bf16[64,1,2,2,16,128]{5,4,3,2,1,0:T(8,128)(2,1)S(1)}, u32[]{:S(2)}, u32[]{:S(2)}) %all-to-all-start.2) | async-done | bytes 1048608 | tf_op jit(solution)/shard_map/all_to_all | solution.py:296
  172.4 0.0 copy-start
  172.4 1.0 copy-done
  173.3 8.9 %attend.5 = bf16[256,8192]{1,0:T(8,128)(2,1)} custom-call(s32[16]{0:T(128)} %lengths_ref.5, s32[64]{0:T(128)} %order_ref.7, s32[1]{0:T(128)} %bitcast.me_ref, bf16[256,8192]{1,0:T(8,128)(2,1)} %q_ref.5, bf16[256,1024]{1,0:T(8,128)(2,1)} %k_own.5, bf16[256,1024]{1,0:T(8,128)(2,1)} %v_own.5, ...), custom_call_target="tpu_custom_call", output_to_operand_aliasing={{}: (7, {})} | custom-call | flops 4831838208 | bytes 2097152 | tf_op jit(solution)/shard_map/attend/pallas_call | solution.py:249
Async XLA Ops:
  107.9 36.8 %all-to-all-start.3 = ((bf16[64,2,2,2,16,128]{5,4,3,2,1,0:T(8,128)(2,1)}), bf16[64,2,2,2,16,128]{5,4,3,2,1,0:T(8,128)(2,1)}, u32[]{:S(2)}, u32[]{:S(2)}) async-start(bf16[64,2,2,2,16,128]{5,4,3,2,1,0:T(8,128)(2,1)} %get-tuple-element.33), calls=%async_computation.3 | async-start | bytes 4194304 | tf_op jit(solution)/shard_map/all_to_all | solution.py:296
  144.6 27.7 %all-to-all-start.2 = ((bf16[64,1,2,2,16,128]{5,4,3,2,1,0:T(8,128)(2,1)}), bf16[64,1,2,2,16,128]{5,4,3,2,1,0:T(8,128)(2,1)S(1)}, u32[]{:S(2)}, u32[]{:S(2)}) async-start(bf16[64,1,2,2,16,128]{5,4,3,2,1,0:T(8,128)(2,1)} %get-tuple-element.32), calls=%async_computation.2 | async-start | bytes 2097152 | tf_op jit(solution)/shard_map/all_to_all | solution.py:296
  172.4 1.0 copy-start

commit v6 on v5

--- a/solution.py
+++ b/solution.py
@@ -12,7 +12,7 @@
 GROUP = 8
 KV_HEADS = 8
 HIDDEN = -1e30
-CHUNKS = ((0, 5), (5, 2), (7, 1))
+FIRST = 11
 THIN = 4
 STACK = 4
 VMEM = 62 << 20
@@ -44,10 +44,17 @@
 
 
 def cut_pieces(own_keys, own_values):
-    blocks = own_keys.shape[0] // THIN
+    rows, width = own_keys.shape
+    blocks = rows // THIN
+    steps = 4
     return pl.pallas_call(
         pieces_kernel,
         out_shape=jax.ShapeDtypeStruct((blocks, KV_HEADS // 2, 16, HEAD), jnp.bfloat16),
+        grid=(steps,),
+        in_specs=[pl.BlockSpec((rows // steps, width), lambda i: (i, 0))] * 2,
+        out_specs=pl.BlockSpec(
+            (blocks // steps, KV_HEADS // 2, 16, HEAD), lambda i: (i, 0, 0, 0)
+        ),
         compiler_params=pltpu.CompilerParams(vmem_limit_bytes=VMEM),
         cost_estimate=pl.CostEstimate(flops=0, bytes_accessed=2 << 20, transcendentals=0),
         name="cut_pieces",
@@ -81,17 +88,16 @@
     def fill(d, carry):
         s = order_ref[step * part + d]
         held = [inverse[jnp.maximum(s - 1 - slot, 0)] for slot in range(past)]
-        for (first, units), out_ref in zip(CHUNKS, out_refs):
-            for c in range(units):
-                h = first + c
-                for tile in range(past // 4):
-                    keys, values = [], []
-                    for slot in (4 * tile, 4 * tile + 2):
-                        near, far = held[slot], held[slot + 1]
-                        keys.append(jnp.where(lower, plain[near, h], rolled[far, h]))
-                        values.append(jnp.where(lower, rolled[near, h], plain[far, h]))
-                    out_ref[d, c, 0, tile] = jnp.concatenate(keys, axis=0).astype(jnp.bfloat16)
-                    out_ref[d, c, 1, tile] = jnp.concatenate(values, axis=0).astype(jnp.bfloat16)
+        for h in range(KV_HEADS):
+            for tile in range(past // 4):
+                keys, values = [], []
+                for slot in (4 * tile, 4 * tile + 2):
+                    near, far = held[slot], held[slot + 1]
+                    keys.append(jnp.where(lower, plain[near, h], rolled[far, h]))
+                    values.append(jnp.where(lower, rolled[near, h], plain[far, h]))
+                for f, rows in ((2 * h, keys), (2 * h + 1, values)):
+                    out_ref, at = (out_refs[0], f) if f < FIRST else (out_refs[1], f - FIRST)
+                    out_ref[d, at, tile] = jnp.concatenate(rows, axis=0).astype(jnp.bfloat16)
         return carry
 
     lax.fori_loop(0, part, fill, 0, unroll=2)
@@ -100,19 +106,17 @@
 def gather_windows(past, block_order, recv):
     blocks = block_order.shape[0]
     part = blocks // 4
-    shape = lambda rows, units: (rows, units, 2, past // 4, 16, HEAD)
+    sizes = (FIRST, 2 * KV_HEADS - FIRST)
+    shape = lambda rows, size: (rows, size, past // 4, 16, HEAD)
     return pl.pallas_call(
         functools.partial(gather_kernel, past),
-        out_shape=[
-            jax.ShapeDtypeStruct(shape(blocks, units), jnp.bfloat16) for _, units in CHUNKS
-        ],
+        out_shape=[jax.ShapeDtypeStruct(shape(blocks, size), jnp.bfloat16) for size in sizes],
         grid_spec=pltpu.PrefetchScalarGridSpec(
             num_scalar_prefetch=1,
             grid=(blocks // part,),
             in_specs=[pl.BlockSpec((blocks, KV_HEADS // 2, 16, HEAD), lambda i, o: (0, 0, 0, 0))],
             out_specs=[
-                pl.BlockSpec(shape(part, units), lambda i, o: (i, 0, 0, 0, 0, 0))
-                for _, units in CHUNKS
+                pl.BlockSpec(shape(part, size), lambda i, o: (i, 0, 0, 0, 0)) for size in sizes
             ],
             scratch_shapes=[
                 pltpu.SMEM((blocks,), jnp.int32),
@@ -120,7 +124,7 @@
                 pltpu.VMEM((blocks, KV_HEADS, 8, HEAD), jnp.float32),
             ],
         ),
-        compiler_params=pltpu.CompilerParams(vmem_limit_bytes=VMEM),
+        compiler_params=pltpu.CompilerParams(vmem_limit_bytes=24 << 20),
         cost_estimate=pl.CostEstimate(flops=0, bytes_accessed=10 << 20, transcendentals=0),
         name="gather_windows",
     )(block_order, recv)
@@ -158,7 +162,7 @@
             keys[to, HEAD:] = pair(*pos, 0.0, HIDDEN)
         return carry
 
-    lax.fori_loop(0, rows // THIN, past, 0, unroll=4)
+    lax.fori_loop(0, rows // THIN, past, 0, unroll=16)
     for r in range(0, rows, 16):
         base = place * rows + r + row
         keys[past_keys + r : past_keys + r + 16, HEAD:] = pair(base, base + 8, 0.0, HIDDEN)
@@ -167,8 +171,9 @@
             stacked[g * rows + r : g * rows + r + 16, HEAD:] = marks
 
 
-def attend_kernel(lengths_ref, order_ref, me_ref, q_ref, k_own, v_own, window, *rest):
+def attend_kernel(early, lengths_ref, order_ref, me_ref, q_ref, k_own, v_own, *rest):
     out_ref, keys, values, stacked, scores_a, scores_b, peak_a, peak_b = rest[-8:]
+    k_window, v_window = rest[:2]
     rows = q_ref.shape[0]
     total_keys = keys.shape[0]
     past_keys = total_keys - rows
@@ -179,9 +184,21 @@
         mark_documents(lengths_ref, order_ref[me_ref[0]], keys, stacked)
         values[:, HEAD:] = jnp.ones((total_keys, HEAD), jnp.bfloat16)
 
-    keys[:past_keys, :HEAD] = window[:, 0, 0].reshape(past_keys, HEAD)
+    if early:
+        keys[:past_keys, :HEAD] = k_window[...].reshape(past_keys, HEAD)
+    else:
+        k_early = rest[2]
+
+        @pl.when(pl.program_id(0) == 0)
+        def _():
+            keys[:past_keys, :HEAD] = k_early[...].reshape(past_keys, HEAD)
+
+        @pl.when(pl.program_id(0) > 0)
+        def _():
+            keys[:past_keys, :HEAD] = k_window[...].reshape(past_keys, HEAD)
+
     keys[past_keys:, :HEAD] = k_own[...]
-    values[:past_keys, :HEAD] = window[:, 0, 1].reshape(past_keys, HEAD)
+    values[:past_keys, :HEAD] = v_window[...].reshape(past_keys, HEAD)
     values[past_keys:, :HEAD] = v_own[...]
     for g in range(GROUP):
         stacked[g * rows : (g + 1) * rows, :HEAD] = q_ref[:, g * HEAD : (g + 1) * HEAD]
@@ -227,27 +244,36 @@
         mix(g, *buffers[g % 2])
 
 
-def attend(first, units, lengths, order, me, queries, own_keys, own_values, window, attended):
+def attend(lengths, order, me, queries, own_keys, own_values, windows, attended):
     rows, width = queries.shape
-    sources, _, _, tiles = window.shape[:4]
+    early = attended is None
+    first = 0 if early else FIRST // 2
+    units = FIRST // 2 if early else KV_HEADS - first
+    sources, _, tiles = windows[0].shape[:3]
     total_keys = sources * tiles * 16 + rows
     tall = STACK * rows
     head = lambda c, *scalars: (0, first + c)
+    half = lambda index: pl.BlockSpec(
+        (sources, 1, tiles, 16, HEAD), lambda c, *scalars: (0, index(c), 0, 0, 0)
+    )
     in_specs = [
         pl.BlockSpec((rows, GROUP * HEAD), head),
         pl.BlockSpec((rows, HEAD), head),
         pl.BlockSpec((rows, HEAD), head),
-        pl.BlockSpec((sources, 1, 2, tiles, 16, HEAD), lambda c, *scalars: (0, c, 0, 0, 0, 0)),
     ]
-    operands = [lengths, order, me, queries, own_keys, own_values, window]
+    operands = [lengths, order, me, queries, own_keys, own_values]
     aliases = {}
-    if attended is not None:
-        in_specs.append(pl.BlockSpec(memory_space=pl.ANY))
-        aliases = {len(operands): 0}
-        operands.append(attended)
+    if early:
+        in_specs += [half(lambda c: 2 * c), half(lambda c: 2 * c + 1)]
+        operands += [windows[0]] * 2
+    else:
+        in_specs += [half(lambda c: jnp.maximum(2 * c - 1, 1)), half(lambda c: 2 * c)]
+        in_specs += [half(lambda c: FIRST - 1), pl.BlockSpec(memory_space=pl.ANY)]
+        operands += [windows[1], windows[1], windows[0], attended]
+        aliases = {len(operands) - 1: 0}
     done = units * GROUP * rows * total_keys
     return pl.pallas_call(
-        attend_kernel,
+        functools.partial(attend_kernel, early),
         out_shape=jax.ShapeDtypeStruct((rows, width), jnp.bfloat16),
         grid_spec=pltpu.PrefetchScalarGridSpec(
             num_scalar_prefetch=3,
@@ -284,18 +310,11 @@
     sends = gather_windows(past, block_order, recv)
     sends, me = lax.optimization_barrier((sends, me))
     window = lax.all_to_all(sends[0], axes, split_axis=0, concat_axis=0, tiled=True)
-    window, me, sends = lax.optimization_barrier((window, me, sends))
+    window, me, send = lax.optimization_barrier((window, me, sends[1]))
+    late = lax.all_to_all(send, axes, split_axis=0, concat_axis=0, tiled=True)
     own = (queries, rotated_key_rows, stored_value_rows)
-    attended = None
-    for step, (first, units) in enumerate(CHUNKS):
-        here = window
-        if step + 1 < len(CHUNKS):
-            send = sends[step + 1]
-            if step:
-                send, attended = lax.optimization_barrier((send, attended))
-            window = lax.all_to_all(send, axes, split_axis=0, concat_axis=0, tiled=True)
-        attended = attend(first, units, doc_lengths, block_order, me, *own, here, attended)
-    return attended
+    attended = attend(doc_lengths, block_order, me, *own, (window,), None)
+    return attend(doc_lengths, block_order, me, *own, (window, late), attended)
 
 
 def solution(mesh):

time: 183 us -> 171 us (0.934)
  starting transfers between devices: 16 us -> 5.74 us
  Pallas kernels: 63.7 us -> 59.5 us
  blocking collectives: 98.8 us -> 103 us
    all_to_all x2 -> x1, starting transfers between devices: 16 us -> 5.74 us  [body(): late = lax.all_to_all(send, axes, split_axis=0, concat_axis=0, tiled=True)]
    all_to_all x1, blocking collectives: 68.4 us -> 72.8 us  [body(): lax.all_to_all(sends[0], axes, split_axis=0, concat_axis=0, tiled=True)]
    pallas_call x3 -> x2, Pallas kernels: 54.7 us -> 51.7 us  [attend(): pl.pallas_call(functools.partial(attend_kernel, early), out_shape=jax.Sha...]
    pallas_call x1, Pallas kernels: 6.65 us -> 4.35 us  [gather_windows(): pl.pallas_call(functools.partial(gather_kernel, past), out_shape=[jax.Sha...]
  transfers between devices with their start and end apart: 2 -> 1, of which waited for: 1 -> 1; matrix products, arithmetic and copies ran while one was open for 0% -> 0% of each run, Pallas kernels for 25% -> 18%
where the time goes in v6:
time: 171 us; the launch traced here: 170 us
  blocking collectives  103 us (60%)
  Pallas kernels  59.5 us (35%)
  starting transfers between devices  5.74 us (3%)
  waiting for transfers between devices  1.94 us (1%)
    all_to_all x1, blocking collectives, body(): lax.all_to_all(sends[0], axes, split_axis=0, concat_axis=0, tiled=True)  72.8 us
    pallas_call x2, Pallas kernels, attend(): pl.pallas_call(functools.partial(attend_kernel, early), out_shape=jax.Sha...  51.7 us
    all_to_all x1, blocking collectives, body(): recv = lax.all_to_all(pieces, axes, split_axis=0, concat_axis=0, tiled=True)  30.3 us
    all_to_all x1, starting transfers between devices, body(): late = lax.all_to_all(send, axes, split_axis=0, concat_axis=0, tiled=True)  5.74 us
    pallas_call x1, Pallas kernels, gather_windows(): pl.pallas_call(functools.partial(gather_kernel, past), out_shape=[jax.Sha...  4.35 us
    pallas_call x1, Pallas kernels, cut_pieces(): pl.pallas_call(pieces_kernel, out_shape=jax.ShapeDtypeStruct((blocks, KV_...  3.51 us
  transfers between devices with their start and end apart: 1, of which 1 were waited for; matrix products, arithmetic and copies ran while one was open for 0% of the time, Pallas kernels for 18%

profile of v6, /device:TPU:0, one launch (start us, length us, event | category | flops | bytes accessed | tf_op | source)
XLA Modules:
  0.0 170.3 jit_solution(16808584417457845180)
XLA Ops:
  0.0 0.0 copy-start
  0.0 3.5 %cut_pieces.1 = bf16[64,4,16,128]{3,2,1,0:T(8,128)(2,1)} custom-call(bf16[256,1024]{1,0:T(8,128)(2,1)} %k_own.3, bf16[256,1024]{1,0:T(8,128)(2,1)} %v_own.3), custom_call_target="tpu_custom_call" | custom-call | bytes 2097152 | tf_op jit(solution)/shard_map/cut_pieces/pallas_call | solution.py:50
  3.5 30.3 %all_to_all.15.recv_ref = bf16[64,4,16,128]{3,2,1,0:T(8,128)(2,1)S(1)} all-to-all(bf16[64,4,16,128]{3,2,1,0:T(8,128)(2,1)} %cut_pieces.1), channel_id=1, replica_groups=mesh['dp'=2,'context'=8,'tensor'=8] {'context','tensor'}, dimensions={0} | all-to-all | bytes 2097152 | tf_op jit(solution)/shard_map/all_to_all | solution.py:309
  33.8 0.0 copy-done
  33.8 4.4 %gather_windows.1 = (bf16[64,11,2,16,128]{4,3,2,1,0:T(8,128)(2,1)S(1)}, bf16[64,5,2,16,128]{4,3,2,1,0:T(8,128)(2,1)}) custom-call(s32[64]{0:T(128)S(1)} %copy-done, bf16[64,4,16,128]{3,2,1,0:T(8,128)(2,1)S(1)} %all_to_all.15.recv_ref), custom_call_target="tpu_custom_call" | custom-call | bytes 10485760 | tf_op jit(solution)/shard_map/gather_windows/pallas_call | solution.py:111
  38.2 72.8 %all_to_all.16.rest_0_.rest_1_.rest_2_ = bf16[64,11,2,16,128]{4,3,2,1,0:T(8,128)(2,1)} all-to-all(bf16[64,11,2,16,128]{4,3,2,1,0:T(8,128)(2,1)S(1)} %get-tuple-element.19), channel_id=1, replica_groups=mesh['dp'=2,'context'=8,'tensor'=8] {'context','tensor'}, dimensions={0} | all-to-all | bytes 11534336 | tf_op jit(solution)/shard_map/all_to_all | solution.py:312
  111.0 5.7 %all-to-all-start.2 = ((bf16[64,5,2,16,128]{4,3,2,1,0:T(8,128)(2,1)}), bf16[64,5,2,16,128]{4,3,2,1,0:T(8,128)(2,1)}, u32[]{:S(2)}, u32[]{:S(2)}) async-start(bf16[64,5,2,16,128]{4,3,2,1,0:T(8,128)(2,1)} %get-tuple-element.23), calls=%async_computation.2 | async-start | bytes 5242880 | tf_op jit(solution)/shard_map/all_to_all | solution.py:314
  116.7 31.3 %attend.2.rest_3_ = bf16[256,8192]{1,0:T(8,128)(2,1)} custom-call(s32[16]{0:T(128)} %lengths_ref.3, s32[64]{0:T(128)} %order_ref.5, s32[1]{0:T(128)} %bitcast.me_ref, bf16[256,8192]{1,0:T(8,128)(2,1)} %q_ref.3, bf16[256,1024]{1,0:T(8,128)(2,1)} %k_own.3, bf16[256,1024]{1,0:T(8,128)(2,1)} %v_own.3, ...), custom_call_target="tpu_custom_call" | custom-call | flops 24159191040 | bytes 10485760 | tf_op jit(solution)/shard_map/attend/pallas_call | solution.py:275
  148.0 1.9 %all-to-all-done.2.rest_0_.rest_1_ = bf16[64,5,2,16,128]{4,3,2,1,0:T(8,128)(2,1)} async-done(((bf16[64,5,2,16,128]{4,3,2,1,0:T(8,128)(2,1)}), bf16[64,5,2,16,128]{4,3,2,1,0:T(8,128)(2,1)}, u32[]{:S(2)}, u32[]{:S(2)}) %all-to-all-start.2) | async-done | bytes 2621472 | tf_op jit(solution)/shard_map/all_to_all | solution.py:314
  149.9 20.4 %attend.3 = bf16[256,8192]{1,0:T(8,128)(2,1)} custom-call(s32[16]{0:T(128)} %lengths_ref.3, s32[64]{0:T(128)} %order_ref.5, s32[1]{0:T(128)} %bitcast.me_ref, bf16[256,8192]{1,0:T(8,128)(2,1)} %q_ref.3, bf16[256,1024]{1,0:T(8,128)(2,1)} %k_own.3, bf16[256,1024]{1,0:T(8,128)(2,1)} %v_own.3, ...), custom_call_target="tpu_custom_call", output_to_operand_aliasing={{}: (9, {})} | custom-call | flops 14495514624 | bytes 6291456 | tf_op jit(solution)/shard_map/attend/pallas_call | solution.py:275
Async XLA Ops:
  0.0 33.8 %copy-start = (s32[64]{0:T(128)S(1)}, s32[64]{0:T(128)}, u32[]{:S(2)}) copy-start(s32[64]{0:T(128)} %order_ref.5) | copy-start | bytes 772
  111.0 39.0 %all-to-all-start.2 = ((bf16[64,5,2,16,128]{4,3,2,1,0:T(8,128)(2,1)}), bf16[64,5,2,16,128]{4,3,2,1,0:T(8,128)(2,1)}, u32[]{:S(2)}, u32[]{:S(2)}) async-start(bf16[64,5,2,16,128]{4,3,2,1,0:T(8,128)(2,1)} %get-tuple-element.23), calls=%async_computation.2 | async-start | bytes 5242880 | tf_op jit(solution)/shard_map/all_to_all | solution.py:314

commit v7 on v6

--- a/solution.py
+++ b/solution.py
@@ -18,9 +18,22 @@
 VMEM = 62 << 20
 
 
-def pieces_kernel(k_ref, v_ref, out_ref):
+def pieces_kernel(k_hbm, v_hbm, out_hbm, k_ref, v_ref, out_ref, sems):
     tall = 16
+    parts = sems.shape[1]
+    part = k_ref.shape[0] // parts
     lower = lax.broadcasted_iota(jnp.int32, (8, HEAD), 0) < THIN
+    copies = []
+    for p in range(parts):
+        rows = pl.ds(p * part, part)
+        copies.append(
+            [
+                pltpu.make_async_copy(hbm.at[rows], held.at[rows], sems.at[i, p])
+                for i, (hbm, held) in enumerate(((k_hbm, k_ref), (v_hbm, v_ref)))
+            ]
+        )
+        for copy in copies[-1]:
+            copy.start()
 
     def some_rows(r, carry):
         rows = pl.ds(pl.multiple_of(r * tall, tall), tall)
@@ -29,64 +42,70 @@
             for h in (2 * pair, 2 * pair + 1):
                 k = k_ref[rows, h * HEAD : (h + 1) * HEAD].astype(jnp.float32)
                 v = v_ref[rows, h * HEAD : (h + 1) * HEAD].astype(jnp.float32)
-                parts = []
+                pieces = []
                 for at in (0, 8):
                     k8, v8 = k[at : at + 8], v[at : at + 8]
-                    parts.append(jnp.where(lower, k8, pltpu.roll(v8, THIN, 0)))
-                    parts.append(jnp.where(lower, pltpu.roll(k8, THIN, 0), v8))
-                halves.append(parts)
+                    pieces.append(jnp.where(lower, k8, pltpu.roll(v8, THIN, 0)))
+                    pieces.append(jnp.where(lower, pltpu.roll(k8, THIN, 0), v8))
+                halves.append(pieces)
             for j in range(tall // THIN):
                 both = jnp.concatenate([halves[0][j], halves[1][j]], axis=0)
                 out_ref[r * (tall // THIN) + j, pair] = both.astype(jnp.bfloat16)
         return carry
 
-    lax.fori_loop(0, k_ref.shape[0] // tall, some_rows, 0, unroll=2)
+    for p in range(parts):
+        for copy in copies[p]:
+            copy.wait()
+        lax.fori_loop(p * part // tall, (p + 1) * part // tall, some_rows, 0, unroll=True)
+        to = pl.ds(p * part // THIN, part // THIN)
+        copies[p].append(pltpu.make_async_copy(out_ref.at[to], out_hbm.at[to], sems.at[2, p]))
+        copies[p][-1].start()
+    for p in range(parts):
+        copies[p][-1].wait()
 
 
 def cut_pieces(own_keys, own_values):
     rows, width = own_keys.shape
     blocks = rows // THIN
-    steps = 4
     return pl.pallas_call(
         pieces_kernel,
         out_shape=jax.ShapeDtypeStruct((blocks, KV_HEADS // 2, 16, HEAD), jnp.bfloat16),
-        grid=(steps,),
-        in_specs=[pl.BlockSpec((rows // steps, width), lambda i: (i, 0))] * 2,
-        out_specs=pl.BlockSpec(
-            (blocks // steps, KV_HEADS // 2, 16, HEAD), lambda i: (i, 0, 0, 0)
-        ),
+        in_specs=[pl.BlockSpec(memory_space=pltpu.HBM)] * 2,
+        out_specs=pl.BlockSpec(memory_space=pltpu.HBM),
+        scratch_shapes=[
+            pltpu.VMEM((rows, width), jnp.bfloat16),
+            pltpu.VMEM((rows, width), jnp.bfloat16),
+            pltpu.VMEM((blocks, KV_HEADS // 2, 16, HEAD), jnp.bfloat16),
+            pltpu.SemaphoreType.DMA((3, 4)),
+        ],
         compiler_params=pltpu.CompilerParams(vmem_limit_bytes=VMEM),
         cost_estimate=pl.CostEstimate(flops=0, bytes_accessed=2 << 20, transcendentals=0),
         name="cut_pieces",
     )(own_keys, own_values)
 
 
-def gather_kernel(past, order_ref, recv_ref, *rest):
-    out_refs, (inverse, plain, rolled) = rest[:-3], rest[-3:]
+def gather_kernel(past, order_ref, recv_ref, early_ref, late_hbm, inverse, plain, rolled, late, sems):
     blocks = order_ref.shape[0]
-    part = out_refs[0].shape[0]
-    step = pl.program_id(0)
+    parts = sems.shape[0]
+    part = blocks // parts
     lower = lax.broadcasted_iota(jnp.int32, (8, HEAD), 0) < THIN
-
-    @pl.when(step == 0)
-    def _():
-        for j in range(blocks):
-            inverse[order_ref[j]] = j
-
-        def open_block(j, carry):
-            for pair in range(KV_HEADS // 2):
-                x = recv_ref[j, pair].astype(jnp.float32)
-                for half in range(2):
-                    h = 2 * pair + half
-                    x8 = x[8 * half : 8 * half + 8]
-                    plain[j, h] = x8
-                    rolled[j, h] = pltpu.roll(x8, THIN, 0)
-            return carry
-
-        lax.fori_loop(0, blocks, open_block, 0, unroll=4)
+    for j in range(blocks):
+        inverse[order_ref[j]] = j
+
+    def open_block(j, carry):
+        for pair in range(KV_HEADS // 2):
+            x = recv_ref[j, pair].astype(jnp.float32)
+            for half in range(2):
+                h = 2 * pair + half
+                x8 = x[8 * half : 8 * half + 8]
+                plain[j, h] = x8
+                rolled[j, h] = pltpu.roll(x8, THIN, 0)
+        return carry
+
+    lax.fori_loop(0, blocks, open_block, 0, unroll=4)
 
     def fill(d, carry):
-        s = order_ref[step * part + d]
+        s = order_ref[d]
         held = [inverse[jnp.maximum(s - 1 - slot, 0)] for slot in range(past)]
         for h in range(KV_HEADS):
             for tile in range(past // 4):
@@ -96,34 +115,45 @@
                     keys.append(jnp.where(lower, plain[near, h], rolled[far, h]))
                     values.append(jnp.where(lower, rolled[near, h], plain[far, h]))
                 for f, rows in ((2 * h, keys), (2 * h + 1, values)):
-                    out_ref, at = (out_refs[0], f) if f < FIRST else (out_refs[1], f - FIRST)
-                    out_ref[d, at, tile] = jnp.concatenate(rows, axis=0).astype(jnp.bfloat16)
+                    to, at = (early_ref, f) if f < FIRST else (late, f - FIRST)
+                    to[d, at, tile] = jnp.concatenate(rows, axis=0).astype(jnp.bfloat16)
         return carry
 
-    lax.fori_loop(0, part, fill, 0, unroll=2)
+    copies = []
+    for p in range(parts):
+        lax.fori_loop(p * part, (p + 1) * part, fill, 0, unroll=2)
+        rows = pl.ds(p * part, part)
+        copies.append(pltpu.make_async_copy(late.at[rows], late_hbm.at[rows], sems.at[p]))
+        copies[-1].start()
+    for copy in copies:
+        copy.wait()
 
 
 def gather_windows(past, block_order, recv):
     blocks = block_order.shape[0]
-    part = blocks // 4
-    sizes = (FIRST, 2 * KV_HEADS - FIRST)
-    shape = lambda rows, size: (rows, size, past // 4, 16, HEAD)
+    shape = lambda size: (blocks, size, past // 4, 16, HEAD)
+    early, late = shape(FIRST), shape(2 * KV_HEADS - FIRST)
     return pl.pallas_call(
         functools.partial(gather_kernel, past),
-        out_shape=[jax.ShapeDtypeStruct(shape(blocks, size), jnp.bfloat16) for size in sizes],
-        grid_spec=pltpu.PrefetchScalarGridSpec(
-            num_scalar_prefetch=1,
-            grid=(blocks // part,),
-            in_specs=[pl.BlockSpec((blocks, KV_HEADS // 2, 16, HEAD), lambda i, o: (0, 0, 0, 0))],
-            out_specs=[
-                pl.BlockSpec(shape(part, size), lambda i, o: (i, 0, 0, 0, 0)) for size in sizes
-            ],
-            scratch_shapes=[
-                pltpu.SMEM((blocks,), jnp.int32),
-                pltpu.VMEM((blocks, KV_HEADS, 8, HEAD), jnp.float32),
-                pltpu.VMEM((blocks, KV_HEADS, 8, HEAD), jnp.float32),
-            ],
-        ),
+        out_shape=[
+            jax.ShapeDtypeStruct(early, jnp.bfloat16),
+            jax.ShapeDtypeStruct(late, jnp.bfloat16),
+        ],
+        in_specs=[
+            pl.BlockSpec(memory_space=pltpu.SMEM),
+            pl.BlockSpec(memory_space=pltpu.VMEM),
+        ],
+        out_specs=[
+            pl.BlockSpec(memory_space=pltpu.VMEM),
+            pl.BlockSpec(memory_space=pltpu.HBM),
+        ],
+        scratch_shapes=[
+            pltpu.SMEM((blocks,), jnp.int32),
+            pltpu.VMEM((blocks, KV_HEADS, 8, HEAD), jnp.float32),
+            pltpu.VMEM((blocks, KV_HEADS, 8, HEAD), jnp.float32),
+            pltpu.VMEM(late, jnp.bfloat16),
+            pltpu.SemaphoreType.DMA((4,)),
+        ],
         compiler_params=pltpu.CompilerParams(vmem_limit_bytes=24 << 20),
         cost_estimate=pl.CostEstimate(flops=0, bytes_accessed=10 << 20, transcendentals=0),
         name="gather_windows",
@@ -173,7 +203,7 @@
 
 def attend_kernel(early, lengths_ref, order_ref, me_ref, q_ref, k_own, v_own, *rest):
     out_ref, keys, values, stacked, scores_a, scores_b, peak_a, peak_b = rest[-8:]
-    k_window, v_window = rest[:2]
+    k_window, v_window = rest[0:2], rest[2:4]
     rows = q_ref.shape[0]
     total_keys = keys.shape[0]
     past_keys = total_keys - rows
@@ -184,21 +214,20 @@
         mark_documents(lengths_ref, order_ref[me_ref[0]], keys, stacked)
         values[:, HEAD:] = jnp.ones((total_keys, HEAD), jnp.bfloat16)
 
+    part = past_keys // 2
+
+    def place_keys(halves):
+        for p, ref in enumerate(halves):
+            keys[p * part : (p + 1) * part, :HEAD] = ref[...].reshape(part, HEAD)
+
     if early:
-        keys[:past_keys, :HEAD] = k_window[...].reshape(past_keys, HEAD)
+        place_keys(k_window)
     else:
-        k_early = rest[2]
-
-        @pl.when(pl.program_id(0) == 0)
-        def _():
-            keys[:past_keys, :HEAD] = k_early[...].reshape(past_keys, HEAD)
-
-        @pl.when(pl.program_id(0) > 0)
-        def _():
-            keys[:past_keys, :HEAD] = k_window[...].reshape(past_keys, HEAD)
-
+        pl.when(pl.program_id(0) == 0)(lambda: place_keys(rest[4:6]))
+        pl.when(pl.program_id(0) > 0)(lambda: place_keys(k_window))
     keys[past_keys:, :HEAD] = k_own[...]
-    values[:past_keys, :HEAD] = v_window[...].reshape(past_keys, HEAD)
+    for p, ref in enumerate(v_window):
+        values[p * part : (p + 1) * part, :HEAD] = ref[...].reshape(part, HEAD)
     values[past_keys:, :HEAD] = v_own[...]
     for g in range(GROUP):
         stacked[g * rows : (g + 1) * rows, :HEAD] = q_ref[:, g * HEAD : (g + 1) * HEAD]
@@ -253,9 +282,13 @@
     total_keys = sources * tiles * 16 + rows
     tall = STACK * rows
     head = lambda c, *scalars: (0, first + c)
-    half = lambda index: pl.BlockSpec(
-        (sources, 1, tiles, 16, HEAD), lambda c, *scalars: (0, index(c), 0, 0, 0)
-    )
+    half = lambda index: [
+        pl.BlockSpec(
+            (sources // 2, 1, tiles, 16, HEAD),
+            lambda c, *scalars, p=p: (p, index(c), 0, 0, 0),
+        )
+        for p in range(2)
+    ]
     in_specs = [
         pl.BlockSpec((rows, GROUP * HEAD), head),
         pl.BlockSpec((rows, HEAD), head),
@@ -264,12 +297,12 @@
     operands = [lengths, order, me, queries, own_keys, own_values]
     aliases = {}
     if early:
-        in_specs += [half(lambda c: 2 * c), half(lambda c: 2 * c + 1)]
-        operands += [windows[0]] * 2
+        in_specs += half(lambda c: 2 * c) + half(lambda c: 2 * c + 1)
+        operands += [windows[0]] * 4
     else:
-        in_specs += [half(lambda c: jnp.maximum(2 * c - 1, 1)), half(lambda c: 2 * c)]
-        in_specs += [half(lambda c: FIRST - 1), pl.BlockSpec(memory_space=pl.ANY)]
-        operands += [windows[1], windows[1], windows[0], attended]
+        in_specs += half(lambda c: jnp.maximum(2 * c - 1, 1)) + half(lambda c: 2 * c)
+        in_specs += half(lambda c: FIRST - 1) + [pl.BlockSpec(memory_space=pl.ANY)]
+        operands += [windows[1]] * 4 + [windows[0]] * 2 + [attended]
         aliases = {len(operands) - 1: 0}
     done = units * GROUP * rows * total_keys
     return pl.pallas_call(

time: 171 us -> 169 us (0.988)
  Pallas kernels: 59.5 us -> 57.7 us
  transfers between devices with their start and end apart: 1 -> 1, of which waited for: 1 -> 1; matrix products, arithmetic and copies ran while one was open for 0% -> 0% of each run, Pallas kernels for 18% -> 19%
where the time goes in v7:
time: 169 us
  blocking collectives  103 us (61%)
  Pallas kernels  57.7 us (34%)
  starting transfers between devices  5.74 us (3%)
  waiting for transfers between devices  1.9 us (1%)
    all_to_all x1, blocking collectives, body(): lax.all_to_all(sends[0], axes, split_axis=0, concat_axis=0, tiled=True)  72.8 us
    pallas_call x2, Pallas kernels, attend(): pl.pallas_call(functools.partial(attend_kernel, early), out_shape=jax.Sha...  51.7 us
    all_to_all x1, blocking collectives, body(): recv = lax.all_to_all(pieces, axes, split_axis=0, concat_axis=0, tiled=True)  30.3 us
    all_to_all x1, starting transfers between devices, body(): late = lax.all_to_all(send, axes, split_axis=0, concat_axis=0, tiled=True)  5.74 us
    pallas_call x1, Pallas kernels, gather_windows(): pl.pallas_call(functools.partial(gather_kernel, past), out_shape=[jax.Sha...  3.81 us
  transfers between devices with their start and end apart: 1, of which 1 were waited for; matrix products, arithmetic and copies ran while one was open for 0% of the time, Pallas kernels for 19%

profile of v7, /device:TPU:0, one launch (start us, length us, event | category | flops | bytes accessed | tf_op | source)
XLA Modules:
  0.0 168.5 jit_solution(15134485649556897216)
XLA Ops:
  0.0 0.0 copy-start
  0.0 2.2 %cut_pieces.1 = bf16[64,4,16,128]{3,2,1,0:T(8,128)(2,1)} custom-call(bf16[256,1024]{1,0:T(8,128)(2,1)} %k_own.3, bf16[256,1024]{1,0:T(8,128)(2,1)} %v_own.3), custom_call_target="tpu_custom_call" | custom-call | bytes 2097152 | tf_op jit(solution)/shard_map/cut_pieces/pallas_call | solution.py:70
  2.2 30.3 %all_to_all.15.recv_ref = bf16[64,4,16,128]{3,2,1,0:T(8,128)(2,1)S(1)} all-to-all(bf16[64,4,16,128]{3,2,1,0:T(8,128)(2,1)} %cut_pieces.1), channel_id=1, replica_groups=mesh['dp'=2,'context'=8,'tensor'=8] {'context','tensor'}, dimensions={0} | all-to-all | bytes 2097152 | tf_op jit(solution)/shard_map/all_to_all | solution.py:342
  32.5 0.0 copy-done
  32.5 3.8 %gather_windows.1 = (bf16[64,11,2,16,128]{4,3,2,1,0:T(8,128)(2,1)S(1)}, bf16[64,5,2,16,128]{4,3,2,1,0:T(8,128)(2,1)}) custom-call(s32[64]{0:T(128)S(1)} %copy-done, bf16[64,4,16,128]{3,2,1,0:T(8,128)(2,1)S(1)} %all_to_all.15.recv_ref), custom_call_target="tpu_custom_call" | custom-call | bytes 10485760 | tf_op jit(solution)/shard_map/gather_windows/pallas_call | solution.py:136
  36.3 72.8 %all_to_all.16.rest_0_.rest_1_.rest_2_.rest_3_.rest_4_.rest_5_ = bf16[64,11,2,16,128]{4,3,2,1,0:T(8,128)(2,1)} all-to-all(bf16[64,11,2,16,128]{4,3,2,1,0:T(8,128)(2,1)S(1)} %get-tuple-element.19), channel_id=1, replica_groups=mesh['dp'=2,'context'=8,'tensor'=8] {'context','tensor'}, dimensions={0} | all-to-all | bytes 11534336 | tf_op jit(solution)/shard_map/all_to_all | solution.py:345
  109.1 5.7 %all-to-all-start.2 = ((bf16[64,5,2,16,128]{4,3,2,1,0:T(8,128)(2,1)}), bf16[64,5,2,16,128]{4,3,2,1,0:T(8,128)(2,1)}, u32[]{:S(2)}, u32[]{:S(2)}) async-start(bf16[64,5,2,16,128]{4,3,2,1,0:T(8,128)(2,1)} %get-tuple-element.23), calls=%async_computation.2 | async-start | bytes 5242880 | tf_op jit(solution)/shard_map/all_to_all | solution.py:347
  114.9 31.3 %attend.2.rest_6_ = bf16[256,8192]{1,0:T(8,128)(2,1)} custom-call(s32[16]{0:T(128)} %lengths_ref.3, s32[64]{0:T(128)} %order_ref.5, s32[1]{0:T(128)} %bitcast.me_ref, bf16[256,8192]{1,0:T(8,128)(2,1)} %q_ref.3, bf16[256,1024]{1,0:T(8,128)(2,1)} %k_own.3, bf16[256,1024]{1,0:T(8,128)(2,1)} %v_own.3, ...), custom_call_target="tpu_custom_call" | custom-call | flops 24159191040 | bytes 10485760 | tf_op jit(solution)/shard_map/attend/pallas_call | solution.py:308
  146.2 1.9 %all-to-all-done.2.rest_0_.rest_1_.rest_2_.rest_3_ = bf16[64,5,2,16,128]{4,3,2,1,0:T(8,128)(2,1)} async-done(((bf16[64,5,2,16,128]{4,3,2,1,0:T(8,128)(2,1)}), bf16[64,5,2,16,128]{4,3,2,1,0:T(8,128)(2,1)}, u32[]{:S(2)}, u32[]{:S(2)}) %all-to-all-start.2) | async-done | bytes 2621472 | tf_op jit(solution)/shard_map/all_to_all | solution.py:347
  148.1 20.4 %attend.3 = bf16[256,8192]{1,0:T(8,128)(2,1)} custom-call(s32[16]{0:T(128)} %lengths_ref.3, s32[64]{0:T(128)} %order_ref.5, s32[1]{0:T(128)} %bitcast.me_ref, bf16[256,8192]{1,0:T(8,128)(2,1)} %q_ref.3, bf16[256,1024]{1,0:T(8,128)(2,1)} %k_own.3, bf16[256,1024]{1,0:T(8,128)(2,1)} %v_own.3, ...), custom_call_target="tpu_custom_call", output_to_operand_aliasing={{}: (12, {})} | custom-call | flops 14495514624 | bytes 6291456 | tf_op jit(solution)/shard_map/attend/pallas_call | solution.py:308
Async XLA Ops:
  0.0 32.5 %copy-start = (s32[64]{0:T(128)S(1)}, s32[64]{0:T(128)}, u32[]{:S(2)}) copy-start(s32[64]{0:T(128)} %order_ref.5) | copy-start | bytes 772
  109.1 39.0 %all-to-all-start.2 = ((bf16[64,5,2,16,128]{4,3,2,1,0:T(8,128)(2,1)}), bf16[64,5,2,16,128]{4,3,2,1,0:T(8,128)(2,1)}, u32[]{:S(2)}, u32[]{:S(2)}) async-start(bf16[64,5,2,16,128]{4,3,2,1,0:T(8,128)(2,1)} %get-tuple-element.23), calls=%async_computation.2 | async-start | bytes 5242880 | tf_op jit(solution)/shard_map/all_to_all | solution.py:347

commit v8 on v7

--- a/solution.py
+++ b/solution.py
@@ -161,7 +161,7 @@
 
 
 def mark_documents(lengths_ref, place, keys, stacked):
-    total_keys, rows = keys.shape[0], stacked.shape[0] // GROUP
+    total_keys, rows = keys.shape[1], stacked.shape[1] // GROUP
     lane = lax.broadcasted_iota(jnp.int32, (8, HEAD), 1)
     row = lax.broadcasted_iota(jnp.int32, (8, HEAD), 0)
     start = jnp.full((8, HEAD), 1 << 30, jnp.int32)
@@ -189,60 +189,103 @@
         for tile in range(slots // 4):
             to = pl.ds(pl.multiple_of((i * (slots // 4) + tile) * 16, 16), 16)
             pos = [origins[2 * tile + half] + i * THIN for half in range(2)]
-            keys[to, HEAD:] = pair(*pos, 0.0, HIDDEN)
+            marks = pair(*pos, 0.0, HIDDEN)
+            for slot in range(2):
+                keys[slot, to, HEAD:] = marks
         return carry
 
     lax.fori_loop(0, rows // THIN, past, 0, unroll=16)
     for r in range(0, rows, 16):
         base = place * rows + r + row
-        keys[past_keys + r : past_keys + r + 16, HEAD:] = pair(base, base + 8, 0.0, HIDDEN)
+        marks = pair(base, base + 8, 0.0, HIDDEN)
+        for slot in range(2):
+            keys[slot, past_keys + r : past_keys + r + 16, HEAD:] = marks
         marks = pair(base, base + 8, 1.0, 0.0)
-        for g in range(GROUP):
-            stacked[g * rows + r : g * rows + r + 16, HEAD:] = marks
-
-
-def attend_kernel(early, lengths_ref, order_ref, me_ref, q_ref, k_own, v_own, *rest):
-    out_ref, keys, values, stacked, scores_a, scores_b, peak_a, peak_b = rest[-8:]
-    k_window, v_window = rest[0:2], rest[2:4]
-    rows = q_ref.shape[0]
-    total_keys = keys.shape[0]
+        for slot in range(2):
+            for g in range(GROUP):
+                stacked[slot, g * rows + r : g * rows + r + 16, HEAD:] = marks
+
+
+def attend_kernel(early, first, units, lengths_ref, order_ref, me_ref, q_hbm, k_hbm, v_hbm, *rest):
+    (out_hbm, keys, values, stacked, scores_a, scores_b, peak_a, peak_b) = rest[-19:-11]
+    (q_held, k_held, v_held, kw_held, vw_held, out_held) = rest[-11:-5]
+    q_sems, own_sems, k_sems, v_sems, out_sems = rest[-5:]
+    rows = q_held.shape[1]
+    total_keys = keys.shape[1]
     past_keys = total_keys - rows
     tall = STACK * rows
-
-    @pl.when(pl.program_id(0) == 0)
-    def _():
-        mark_documents(lengths_ref, order_ref[me_ref[0]], keys, stacked)
-        values[:, HEAD:] = jnp.ones((total_keys, HEAD), jnp.bfloat16)
-
-    part = past_keys // 2
-
-    def place_keys(halves):
-        for p, ref in enumerate(halves):
-            keys[p * part : (p + 1) * part, :HEAD] = ref[...].reshape(part, HEAD)
-
-    if early:
-        place_keys(k_window)
-    else:
-        pl.when(pl.program_id(0) == 0)(lambda: place_keys(rest[4:6]))
-        pl.when(pl.program_id(0) > 0)(lambda: place_keys(k_window))
-    keys[past_keys:, :HEAD] = k_own[...]
-    for p, ref in enumerate(v_window):
-        values[p * part : (p + 1) * part, :HEAD] = ref[...].reshape(part, HEAD)
-    values[past_keys:, :HEAD] = v_own[...]
-    for g in range(GROUP):
-        stacked[g * rows : (g + 1) * rows, :HEAD] = q_ref[:, g * HEAD : (g + 1) * HEAD]
+    wide = STACK * HEAD
+    stacks = GROUP // STACK
+    window = rest[0]
+
+    def columns(c, width, part=0):
+        at = (first + c) * GROUP * HEAD + part * wide if width == wide else (first + c) * HEAD
+        return pl.ds(pl.multiple_of(at, HEAD), width)
+
+    def q_copy(c, slot, part):
+        return pltpu.make_async_copy(
+            q_hbm.at[:, columns(c, wide, part)],
+            q_held.at[slot, :, pl.ds(part * wide, wide)],
+            q_sems.at[slot, part],
+        )
+
+    def own_copy(c, slot, i):
+        hbm, held = ((k_hbm, k_held), (v_hbm, v_held))[i]
+        return pltpu.make_async_copy(
+            hbm.at[:, columns(c, HEAD)], held.at[slot], own_sems.at[slot, i]
+        )
+
+    def k_copy(c, slot):
+        at = 2 * c if early else jnp.maximum(2 * c - 1, 0)
+        return pltpu.make_async_copy(window.at[:, at], kw_held.at[slot], k_sems.at[slot])
+
+    def v_copy(c, slot):
+        at = 2 * c + 1 if early else 2 * c
+        return pltpu.make_async_copy(window.at[:, at], vw_held.at[slot], v_sems.at[slot])
+
+    def out_copy(c, slot, part):
+        return pltpu.make_async_copy(
+            out_held.at[slot, :, pl.ds(part * wide, wide)],
+            out_hbm.at[:, columns(c, wide, part)],
+            out_sems.at[slot, part],
+        )
+
+    def start_front(c, slot, copy=None):
+        (copy or k_copy(c, slot)).start()
+        own_copy(c, slot, 0).start()
+        for part in range(stacks):
+            q_copy(c, slot, part).start()
+
+    def wait_front(c, slot):
+        k_copy(c, slot).wait()
+        own_copy(c, slot, 0).wait()
+        for part in range(stacks):
+            q_copy(c, slot, part).wait()
+
+    def start_back(c, slot):
+        own_copy(c, slot, 1).start()
+        v_copy(c, slot).start()
+
+    begin = None
+    if not early:
+        begin = pltpu.make_async_copy(rest[1].at[:, FIRST - 1], kw_held.at[0], k_sems.at[0])
+    start_front(0, 0, begin)
+    start_back(0, 0)
+    start_front(1, 1)
+    mark_documents(lengths_ref, order_ref[me_ref[0]], keys, stacked)
+    values[:, HEAD:] = jnp.ones((total_keys, HEAD), jnp.bfloat16)
     scale = math.log2(math.e) / math.sqrt(HEAD)
     tiles = [(t, t + rows) for t in range(0, total_keys, rows)]
     causal = lax.broadcasted_iota(jnp.int32, (tall, rows), 0) % rows >= lax.broadcasted_iota(
         jnp.int32, (tall, rows), 1
     )
 
-    def score(g, scores, peak):
-        q = stacked[g * tall : (g + 1) * tall, :]
+    def score(g, scores, peak, slot):
+        q = stacked[slot, g * tall : (g + 1) * tall, :]
         most = None
         for a, b in tiles:
             s = lax.dot_general(
-                q, keys[a:b, :], (((1,), (1,)), ((), ())), preferred_element_type=jnp.float32
+                q, keys[slot, a:b, :], (((1,), (1,)), ((), ())), preferred_element_type=jnp.float32
             )
             if a == past_keys:
                 s = jnp.where(causal, s, HIDDEN)
@@ -252,7 +295,7 @@
                 most = part if most is None else jnp.maximum(most, part)
         peak[...] = jnp.broadcast_to(jnp.max(most, axis=1, keepdims=True), (tall, HEAD))
 
-    def mix(g, scores, peak):
+    def mix(g, scores, peak, slot):
         most = jnp.concatenate([peak[...]] * (rows // HEAD), axis=1)
         mixed = None
         for a, b in tiles:
@@ -262,15 +305,66 @@
         out = (mixed[:, :HEAD] / mixed[:, HEAD:]).astype(jnp.bfloat16)
         for h in range(STACK):
             at = (g * STACK + h) * HEAD
-            out_ref[:, at : at + HEAD] = out[h * rows : (h + 1) * rows]
-
-    buffers = ((scores_a, peak_a), (scores_b, peak_b))
-    stacks = GROUP // STACK
-    score(0, *buffers[0])
-    for g in range(stacks):
-        if g + 1 < stacks:
-            score(g + 1, *buffers[(g + 1) % 2])
-        mix(g, *buffers[g % 2])
+            out_held[slot, :, at : at + HEAD] = out[h * rows : (h + 1) * rows]
+
+    first_buffer, second_buffer = (scores_a, peak_a), (scores_b, peak_b)
+
+    def build_front(slot):
+        keys[slot, :past_keys, :HEAD] = kw_held[slot].reshape(past_keys, HEAD)
+        keys[slot, past_keys:, :HEAD] = k_held[slot]
+        for g in range(GROUP):
+            q = q_held[slot, :, g * HEAD : (g + 1) * HEAD]
+            stacked[slot, g * rows : (g + 1) * rows, :HEAD] = q
+
+    def build_back(slot):
+        values[:past_keys, :HEAD] = vw_held[slot].reshape(past_keys, HEAD)
+        values[past_keys:, :HEAD] = v_held[slot]
+
+    def wait_back(c, slot):
+        own_copy(c, slot, 1).wait()
+        v_copy(c, slot).wait()
+
+    def wait_out(c, slot):
+        for part in range(stacks):
+            out_copy(c, slot, part).wait()
+
+    def start_out(c, slot):
+        for part in range(stacks):
+            out_copy(c, slot, part).start()
+
+    def one_head(c, carry):
+        slot = lax.rem(c, 2)
+        other = 1 - slot
+        wait_back(c, slot)
+        wait_front(c + 1, other)
+        pl.when(c + 2 < units)(lambda: start_front(c + 2, slot))
+        start_back(c + 1, other)
+        pl.when(c >= 2)(lambda: wait_out(c - 2, slot))
+        build_back(slot)
+        build_front(other)
+        score(1, *second_buffer, slot)
+        mix(0, *first_buffer, slot)
+        score(0, *first_buffer, other)
+        mix(1, *second_buffer, slot)
+        start_out(c, slot)
+        return carry
+
+    wait_front(0, 0)
+    build_front(0)
+    score(0, *first_buffer, 0)
+    lax.fori_loop(0, units - 1, one_head, 0)
+    c = units - 1
+    slot = c % 2
+    wait_back(c, slot)
+    if c >= 2:
+        wait_out(c - 2, slot)
+    build_back(slot)
+    score(1, *second_buffer, slot)
+    mix(0, *first_buffer, slot)
+    mix(1, *second_buffer, slot)
+    start_out(c, slot)
+    wait_out(c - 1, 1 - slot)
+    wait_out(c, slot)
 
 
 def attend(lengths, order, me, queries, own_keys, own_values, windows, attended):
@@ -281,49 +375,37 @@
     sources, _, tiles = windows[0].shape[:3]
     total_keys = sources * tiles * 16 + rows
     tall = STACK * rows
-    head = lambda c, *scalars: (0, first + c)
-    half = lambda index: [
-        pl.BlockSpec(
-            (sources // 2, 1, tiles, 16, HEAD),
-            lambda c, *scalars, p=p: (p, index(c), 0, 0, 0),
-        )
-        for p in range(2)
-    ]
-    in_specs = [
-        pl.BlockSpec((rows, GROUP * HEAD), head),
-        pl.BlockSpec((rows, HEAD), head),
-        pl.BlockSpec((rows, HEAD), head),
-    ]
+    smem, hbm = pl.BlockSpec(memory_space=pltpu.SMEM), pl.BlockSpec(memory_space=pl.ANY)
     operands = [lengths, order, me, queries, own_keys, own_values]
-    aliases = {}
-    if early:
-        in_specs += half(lambda c: 2 * c) + half(lambda c: 2 * c + 1)
-        operands += [windows[0]] * 4
-    else:
-        in_specs += half(lambda c: jnp.maximum(2 * c - 1, 1)) + half(lambda c: 2 * c)
-        in_specs += half(lambda c: FIRST - 1) + [pl.BlockSpec(memory_space=pl.ANY)]
-        operands += [windows[1]] * 4 + [windows[0]] * 2 + [attended]
-        aliases = {len(operands) - 1: 0}
+    operands += [windows[0]] if early else [windows[1], windows[0], attended]
+    held = lambda *shape: pltpu.VMEM((2, *shape), jnp.bfloat16)
     done = units * GROUP * rows * total_keys
     return pl.pallas_call(
-        functools.partial(attend_kernel, early),
+        functools.partial(attend_kernel, early, first, units),
         out_shape=jax.ShapeDtypeStruct((rows, width), jnp.bfloat16),
-        grid_spec=pltpu.PrefetchScalarGridSpec(
-            num_scalar_prefetch=3,
-            grid=(units,),
-            in_specs=in_specs,
-            out_specs=pl.BlockSpec((rows, GROUP * HEAD), head),
-            scratch_shapes=[
-                pltpu.VMEM((total_keys, 2 * HEAD), jnp.bfloat16),
-                pltpu.VMEM((total_keys, 2 * HEAD), jnp.bfloat16),
-                pltpu.VMEM((GROUP * rows, 2 * HEAD), jnp.bfloat16),
-                pltpu.VMEM((tall, total_keys), jnp.float32),
-                pltpu.VMEM((tall, total_keys), jnp.float32),
-                pltpu.VMEM((tall, HEAD), jnp.float32),
-                pltpu.VMEM((tall, HEAD), jnp.float32),
-            ],
-        ),
-        input_output_aliases=aliases,
+        in_specs=[smem] * 3 + [hbm] * (len(operands) - 3),
+        out_specs=hbm,
+        scratch_shapes=[
+            held(total_keys, 2 * HEAD),
+            pltpu.VMEM((total_keys, 2 * HEAD), jnp.bfloat16),
+            held(GROUP * rows, 2 * HEAD),
+            pltpu.VMEM((tall, total_keys), jnp.float32),
+            pltpu.VMEM((tall, total_keys), jnp.float32),
+            pltpu.VMEM((tall, HEAD), jnp.float32),
+            pltpu.VMEM((tall, HEAD), jnp.float32),
+            held(rows, GROUP * HEAD),
+            held(rows, HEAD),
+            held(rows, HEAD),
+            held(sources, tiles, 16, HEAD),
+            held(sources, tiles, 16, HEAD),
+            held(rows, GROUP * HEAD),
+            pltpu.SemaphoreType.DMA((2, GROUP // STACK)),
+            pltpu.SemaphoreType.DMA((2, 2)),
+            pltpu.SemaphoreType.DMA((2,)),
+            pltpu.SemaphoreType.DMA((2,)),
+            pltpu.SemaphoreType.DMA((2, GROUP // STACK)),
+        ],
+        input_output_aliases={} if early else {len(operands) - 1: 0},
         compiler_params=pltpu.CompilerParams(vmem_limit_bytes=VMEM),
         cost_estimate=pl.CostEstimate(
             flops=done * 2 * 4 * HEAD, bytes_accessed=units << 21, transcendentals=done

time: 169 us -> 168 us (level)
  Pallas kernels: 57.7 us -> 55.8 us
    pallas_call x2, Pallas kernels: 51.7 us -> 49.8 us  [attend(): pl.pallas_call(functools.partial(attend_kernel, early, first, units), out...]
  transfers between devices with their start and end apart: 1 -> 1, of which waited for: 1 -> 1; matrix products, arithmetic and copies ran while one was open for 0% -> 0% of each run, Pallas kernels for 19% -> 18%
where the time goes in v8:
time: 168 us
  blocking collectives  103 us (61%)
  Pallas kernels  55.8 us (33%)
  starting transfers between devices  5.74 us (3%)
  waiting for transfers between devices  2.9 us (2%)
    all_to_all x1, blocking collectives, body(): lax.all_to_all(sends[0], axes, split_axis=0, concat_axis=0, tiled=True)  72.8 us
    pallas_call x2, Pallas kernels, attend(): pl.pallas_call(functools.partial(attend_kernel, early, first, units), out...  49.8 us
    all_to_all x1, blocking collectives, body(): recv = lax.all_to_all(pieces, axes, split_axis=0, concat_axis=0, tiled=True)  30.3 us
    all_to_all x1, starting transfers between devices, body(): late = lax.all_to_all(send, axes, split_axis=0, concat_axis=0, tiled=True)  5.74 us
    pallas_call x1, Pallas kernels, gather_windows(): pl.pallas_call(functools.partial(gather_kernel, past), out_shape=[jax.Sha...  3.81 us
  transfers between devices with their start and end apart: 1, of which 1 were waited for; matrix products, arithmetic and copies ran while one was open for 0% of the time, Pallas kernels for 18%

profile of v8, /device:TPU:0, one launch (start us, length us, event | category | flops | bytes accessed | tf_op | source)
XLA Modules:
  0.0 167.7 jit_solution(5034433929641077424)
XLA Ops:
  0.0 0.0 copy-start
  0.0 2.2 %cut_pieces.1 = bf16[64,4,16,128]{3,2,1,0:T(8,128)(2,1)} custom-call(bf16[256,1024]{1,0:T(8,128)(2,1)} %k_hbm.5, bf16[256,1024]{1,0:T(8,128)(2,1)} %v_hbm.5), custom_call_target="tpu_custom_call" | custom-call | bytes 2097152 | tf_op jit(solution)/shard_map/cut_pieces/pallas_call | solution.py:70
  2.2 30.3 %all_to_all.15.recv_ref = bf16[64,4,16,128]{3,2,1,0:T(8,128)(2,1)S(1)} all-to-all(bf16[64,4,16,128]{3,2,1,0:T(8,128)(2,1)} %cut_pieces.1), channel_id=1, replica_groups=mesh['dp'=2,'context'=8,'tensor'=8] {'context','tensor'}, dimensions={0} | all-to-all | bytes 2097152 | tf_op jit(solution)/shard_map/all_to_all | solution.py:424
  32.5 0.0 copy-done
  32.5 3.8 %gather_windows.1 = (bf16[64,11,2,16,128]{4,3,2,1,0:T(8,128)(2,1)S(1)}, bf16[64,5,2,16,128]{4,3,2,1,0:T(8,128)(2,1)}) custom-call(s32[64]{0:T(128)S(1)} %copy-done, bf16[64,4,16,128]{3,2,1,0:T(8,128)(2,1)S(1)} %all_to_all.15.recv_ref), custom_call_target="tpu_custom_call" | custom-call | bytes 10485760 | tf_op jit(solution)/shard_map/gather_windows/pallas_call | solution.py:136
  36.3 72.8 %all_to_all.16.rest_0_.rest_1_ = bf16[64,11,2,16,128]{4,3,2,1,0:T(8,128)(2,1)} all-to-all(bf16[64,11,2,16,128]{4,3,2,1,0:T(8,128)(2,1)S(1)} %get-tuple-element.19), channel_id=1, replica_groups=mesh['dp'=2,'context'=8,'tensor'=8] {'context','tensor'}, dimensions={0} | all-to-all | bytes 11534336 | tf_op jit(solution)/shard_map/all_to_all | solution.py:427
  109.1 5.7 %all-to-all-start.2 = ((bf16[64,5,2,16,128]{4,3,2,1,0:T(8,128)(2,1)}), bf16[64,5,2,16,128]{4,3,2,1,0:T(8,128)(2,1)}, u32[]{:S(2)}, u32[]{:S(2)}) async-start(bf16[64,5,2,16,128]{4,3,2,1,0:T(8,128)(2,1)} %get-tuple-element.23), calls=%async_computation.2 | async-start | bytes 5242880 | tf_op jit(solution)/shard_map/all_to_all | solution.py:429
  114.9 30.3 %attend.2.rest_2_ = bf16[256,8192]{1,0:T(8,128)(2,1)} custom-call(s32[16]{0:T(128)} %lengths_ref.3, s32[64]{0:T(128)} %order_ref.5, s32[1]{0:T(128)} %bitcast.me_ref, bf16[256,8192]{1,0:T(8,128)(2,1)} %q_hbm.3, bf16[256,1024]{1,0:T(8,128)(2,1)} %k_hbm.5, bf16[256,1024]{1,0:T(8,128)(2,1)} %v_hbm.5, bf16[64,11,2,16,128]{4,3,2,1,0:T(8,128)(2,1)} %all_to_all.16.rest_0_.rest_1_), custom_call_target="tpu_custom_call" | custom-call | flops 24159191040 | bytes 10485760 | tf_op jit(solution)/shard_map/attend/pallas_call | solution.py:383
  145.2 2.9 %all-to-all-done.2.rest_0_ = bf16[64,5,2,16,128]{4,3,2,1,0:T(8,128)(2,1)} async-done(((bf16[64,5,2,16,128]{4,3,2,1,0:T(8,128)(2,1)}), bf16[64,5,2,16,128]{4,3,2,1,0:T(8,128)(2,1)}, u32[]{:S(2)}, u32[]{:S(2)}) %all-to-all-start.2) | async-done | bytes 2621472 | tf_op jit(solution)/shard_map/all_to_all | solution.py:429
  148.1 19.5 %attend.3 = bf16[256,8192]{1,0:T(8,128)(2,1)} custom-call(s32[16]{0:T(128)} %lengths_ref.3, s32[64]{0:T(128)} %order_ref.5, s32[1]{0:T(128)} %bitcast.me_ref, bf16[256,8192]{1,0:T(8,128)(2,1)} %q_hbm.3, bf16[256,1024]{1,0:T(8,128)(2,1)} %k_hbm.5, bf16[256,1024]{1,0:T(8,128)(2,1)} %v_hbm.5, ...), custom_call_target="tpu_custom_call", output_to_operand_aliasing={{}: (8, {})} | custom-call | flops 14495514624 | bytes 6291456 | tf_op jit(solution)/shard_map/attend/pallas_call | solution.py:383
Async XLA Ops:
  0.0 32.5 %copy-start = (s32[64]{0:T(128)S(1)}, s32[64]{0:T(128)}, u32[]{:S(2)}) copy-start(s32[64]{0:T(128)} %order_ref.5) | copy-start | bytes 772
  109.1 39.0 %all-to-all-start.2 = ((bf16[64,5,2,16,128]{4,3,2,1,0:T(8,128)(2,1)}), bf16[64,5,2,16,128]{4,3,2,1,0:T(8,128)(2,1)}, u32[]{:S(2)}, u32[]{:S(2)}) async-start(bf16[64,5,2,16,128]{4,3,2,1,0:T(8,128)(2,1)} %get-tuple-element.23), calls=%async_computation.2 | async-start | bytes 5242880 | tf_op jit(solution)/shard_map/all_to_all | solution.py:429
